TPU v7x, 32 devices: a whole 2x2x4 slice. The times are simulated.
32 devices in a mesh: tm: 2 (over core), uv: 16 (over z, y, x).
Axes of the slice: x: 2, y: 2, z: 4, core: 2. Of those that a mesh axis runs over, the one named last changes fastest.
Arguments:
- visibilities: bfloat16 [8, 16, 2, 2, 32768], P(None, 'tm', None, None, 'uv'), may hold values from -6 to 6
- u_offset: float32 [2, 8, 32768], P('tm', None, 'uv'), may hold values from 0 to 128
- v_offset: float32 [2, 8, 32768], P('tm', None, 'uv'), may hold values from 0 to 512
- block_owner: int32 [2, 2048, 1], P('tm', 'uv'), may hold values from 0 to 15; in each aligned block of 128 rows (0 to 127, 128 to 255, ..., all dimensions but the last counted through in order) at most 24 rows name the same one
- block_u_tile: int32 [2, 2048], P('tm', 'uv'), may hold values from 0 to 63
- block_count: int32 [2, 2048], P('tm', 'uv'), may hold values from 16 to 128
- sk_window: int32 [2, 2], P('tm'), may hold values from 300 to 2200, as said below
Outputs:
- dirty_image: float32 [2, 4096, 4096], P('tm', 'uv')
Inputs may be any that keep to these rules, and one draw needn't show every extreme that they name: `block_owner`: in each channel, the blocks of one index of uv name no band more than 24 times, a bound that some block reaches. `sk_window`: the lower limit lies from 300 to 600 and the upper from 1600 to 2200; in every draw some channel's lower limit is exactly 300 and some channel's upper limit exactly 2200.
All inputs are finite; a program needn't handle non-finite values.
Results may differ from a plain program's by a relative error of at most 0.0053.
Values sent between devices are 32-bit elements; how exact they have to be, the bound alone decides.
A program may use at most 128 MiB of HBM per device.

v0:
```python
import math

import jax
import jax.numpy as jnp
from jax import lax
from jax.sharding import PartitionSpec as P

NG = 8192
TILE = 128
VISIBILITY_ROWS = 128
SUBS = 16
NBIN = 8
BL_DEV = 2048
NI = 4096


kernel_width = 1.3
ramp_width = 0.25


def kurtosis_weight(first_sum, second, window):
    ratio = SUBS * second / (first_sum * first_sum)
    kurtosis = (SUBS + 1.0) / (SUBS - 1.0) * (ratio - 1.0)
    lower = window[0].astype(jnp.float32) / 1000.0
    upper = window[1].astype(jnp.float32) / 1000.0
    return jnp.clip((kurtosis - lower) / ramp_width, 0.0, 1.0) * jnp.clip(
        (upper - kurtosis) / ramp_width, 0.0, 1.0
    )


def grid_tiles(payload, band_rows):
    rows_v = jnp.arange(band_rows).astype(jnp.float32)
    cols_u = jnp.arange(TILE).astype(jnp.float32)
    gap_v = rows_v[None, None, :] - payload[:, 3, :, None]
    gap_u = cols_u[None, None, :] - payload[:, 2, :, None]
    left = jnp.exp(-0.5 * gap_v * gap_v / (kernel_width * kernel_width)).astype(jnp.bfloat16)
    across = jnp.exp(-0.5 * gap_u * gap_u / (kernel_width * kernel_width))
    right = jnp.concatenate(
        [payload[:, 0, :, None] * across, payload[:, 1, :, None] * across], axis=2
    ).astype(jnp.bfloat16)
    return jnp.einsum("grj,gri->gji", left, right, preferred_element_type=jnp.float32)


def taper(indices):
    offset = indices.astype(jnp.float32) - NI // 2
    scaled = offset / NG
    return jnp.exp(-2.0 * math.pi * math.pi * kernel_width * kernel_width * scaled * scaled)


def angle_table(row_ids, col_ids, modulus):
    product = row_ids[:, None] * col_ids[None, :] % modulus
    angles = product.astype(jnp.float32) * (2.0 * math.pi / modulus)
    return (jnp.cos(angles), jnp.sin(angles))


def make_tables():
    outer = NG // TILE
    kept = NI // outer
    select = jnp.concatenate([jnp.arange(TILE - kept // 2, TILE), jnp.arange(0, kept // 2)])
    section_one = angle_table(jnp.arange(outer), jnp.arange(outer), outer)
    twiddle = angle_table(jnp.arange(outer), jnp.arange(TILE), NG)
    section_three = angle_table(jnp.arange(TILE), select, TILE)
    return (section_one, twiddle, section_three)


def complex_mix(subscripts, factors, real_part, imag_part, real_only):
    cos_part, sin_part = factors

    def mixed(values, weights):
        return jnp.einsum(subscripts, values, weights, precision=lax.Precision.HIGHEST)

    out_real = mixed(real_part, cos_part) - mixed(imag_part, sin_part)
    if real_only:
        return (out_real, None)
    return (out_real, mixed(real_part, sin_part) + mixed(imag_part, cos_part))


def twist(real_part, imag_part, factors):
    cos_part, sin_part = factors
    return (
        real_part * cos_part - imag_part * sin_part,
        real_part * sin_part + imag_part * cos_part,
    )


def dft_tiled(real_part, imag_part, tables):
    section_one, twiddle, section_three = tables
    rows_out = real_part.shape[1]
    first_real, first_imag = complex_mix("nrq,kn->rkq", section_one, real_part, imag_part, False)
    cos_part, sin_part = twiddle
    first_real, first_imag = twist(first_real, first_imag, (cos_part[None], sin_part[None]))
    out_real, out_imag = complex_mix("rkq,qj->rjk", section_three, first_real, first_imag, False)
    return (out_real.reshape(rows_out, NI), out_imag.reshape(rows_out, NI))


def dft_middle(real_part, imag_part, tables):
    section_one, twiddle, section_three = tables
    outer = NG // TILE
    leading = real_part.shape[0]
    trailing = real_part.shape[2]
    shaped_real = real_part.reshape(leading, outer, TILE, trailing)
    shaped_imag = imag_part.reshape(leading, outer, TILE, trailing)
    first_real, first_imag = complex_mix(
        "anqb,kn->akqb", section_one, shaped_real, shaped_imag, False
    )
    cos_part, sin_part = twiddle
    first_real, first_imag = twist(
        first_real, first_imag, (cos_part[None, :, :, None], sin_part[None, :, :, None])
    )
    out_real, out_imag = complex_mix("akqb,qj->ajkb", section_three, first_real, first_imag, True)
    return (out_real.reshape(leading, NI, trailing), None)


def finish(values, row_ids, col_ids, scale):
    sign_flip = 1.0 - 2.0 * ((row_ids[:, None] + col_ids[None, :]) % 2).astype(jnp.float32)
    return values * sign_flip * scale / (taper(row_ids)[:, None] * taper(col_ids)[None, :])


def body(visibilities, u_offset, v_offset, block_owner, block_u_tile, block_count, sk_window):
    owners = lax.axis_size("uv")
    local_bin_count = visibilities.shape[0]
    antenna_pairs = visibilities.shape[4]
    local_block_count = local_bin_count * antenna_pairs // VISIBILITY_ROWS
    real_part = visibilities[:, :, :, 0].astype(jnp.float32)
    imag_part = visibilities[:, :, :, 1].astype(jnp.float32)
    powers = real_part * real_part + imag_part * imag_part
    local_sums = jnp.stack(
        [
            jnp.sum(real_part, axis=1),
            jnp.sum(imag_part, axis=1),
            jnp.sum(powers, axis=1),
            jnp.sum(powers * powers, axis=1),
        ],
        axis=0,
    )
    local_sums = local_sums.transpose(2, 0, 1, 3)
    totals = lax.psum_scatter(local_sums, "tm", scatter_dimension=0, tiled=True)[0]
    weight = kurtosis_weight(totals[2], totals[3], sk_window[0])
    avg_real = (weight * totals[0] / SUBS).reshape(local_block_count, VISIBILITY_ROWS)
    avg_imag = (weight * totals[1] / SUBS).reshape(local_block_count, VISIBILITY_ROWS)
    live_rows = jnp.arange(VISIBILITY_ROWS)[None, :] < block_count[0][:, None]
    avg_real = jnp.where(live_rows, avg_real, 0.0)
    avg_imag = jnp.where(live_rows, avg_imag, 0.0)
    payload = jnp.stack(
        [
            avg_real,
            avg_imag,
            u_offset[0].reshape(local_block_count, VISIBILITY_ROWS),
            v_offset[0].reshape(local_block_count, VISIBILITY_ROWS),
        ],
        axis=1,
    )
    owner_ids = block_owner[0, :, 0]
    capacity = 3 * local_block_count // owners
    onehot = (owner_ids[:, None] == jnp.arange(owners)[None, :]).astype(jnp.int32)
    before = jnp.cumsum(onehot, axis=0) - onehot
    slot_rank = jnp.sum(before * onehot, axis=1)
    target = owner_ids * capacity + slot_rank
    slot_total = owners * capacity
    outgoing = jnp.zeros((slot_total, 4, VISIBILITY_ROWS), jnp.float32).at[target].set(payload)
    outgoing_tiles = jnp.zeros((slot_total,), jnp.int32).at[target].set(block_u_tile[0])
    received, received_tiles = (
        lax.all_to_all(
            outgoing.reshape(owners, capacity, 4, VISIBILITY_ROWS),
            "uv",
            split_axis=0,
            concat_axis=0,
            tiled=True,
        ),
        lax.all_to_all(
            outgoing_tiles.reshape(owners, capacity), "uv", split_axis=0, concat_axis=0, tiled=True
        ),
    )
    band_rows = NG // owners
    tile_count = NG // TILE
    group_size = math.gcd(slot_total, 64)

    def accumulate(running, pieces):
        message_group, tile_group = pieces
        return (running.at[tile_group].add(grid_tiles(message_group, band_rows)), None)

    uv_grid = jnp.zeros((tile_count, band_rows, 2 * TILE), jnp.float32)
    uv_grid, _ = lax.scan(
        accumulate,
        uv_grid,
        (
            received.reshape(-1, group_size, 4, VISIBILITY_ROWS),
            received_tiles.reshape(-1, group_size),
        ),
    )
    grid_real = uv_grid[:, :, :TILE]
    grid_imag = uv_grid[:, :, TILE:]
    tables = make_tables()
    scale = 1.0 / math.sqrt(NBIN * BL_DEV * owners)
    rows_mine = NI // owners
    pixel_ids = jnp.arange(NI)
    mine_ids = lax.axis_index("uv") * rows_mine + jnp.arange(rows_mine)
    half_real, half_imag = dft_tiled(grid_real, grid_imag, tables)
    column_real, column_imag = (
        lax.all_to_all(half_real, "uv", split_axis=1, concat_axis=0, tiled=True),
        lax.all_to_all(half_imag, "uv", split_axis=1, concat_axis=0, tiled=True),
    )
    sky_image, _ = dft_middle(column_real[None], column_imag[None], tables)
    finished = finish(sky_image[0], pixel_ids, mine_ids, scale)
    dirty_image = lax.all_to_all(finished, "uv", split_axis=0, concat_axis=1, tiled=True)
    return dirty_image[None]


def solution(mesh):
    placed = (
        P(None, "tm", None, None, "uv"),
        P("tm", None, "uv"),
        P("tm", None, "uv"),
        P("tm", "uv", None),
        P("tm", "uv"),
        P("tm", "uv"),
        P("tm", None),
    )
    return jax.shard_map(
        body, mesh=mesh, in_specs=placed, out_specs=P("tm", "uv", None), check_vma=False
    )
```

profile of v0, /device:TPU:14, one launch (start us, length us, event | category | flops | bytes accessed | tf_op | source)
XLA Modules:
  0.0 1388.1 jit_solution(3116607991733767740)
XLA Ops:
  6.5 5.1 convert_reduce_fusion.1
  19.1 7.1 all-to-all-start
  32.1 4.3 scatter_fusion.1
  37.4 7.2 all-to-all-start.1
  47.4 15.2 %all-to-all-done.1 = f32[16,24,4,128]{3,1,2,0:T(8,128)S(1)} async-done(((f32[16,24,4,128]{3,1,2,0:T(8,128)}), f32[16,24,4,128]{3,1,2,0:T(8,128)S(1)}, u32[]{:S(2)}, u32[]{:S(2)}) %all-to-all-start.1) | async-done | bytes 786464 | tf_op jit(solution)/shard_map/all_to_all | solution.py:163
  62.7 11.1 broadcast_in_dim.11
  73.8 511.0 %while.10 = (s32[]{:T(128)}, f32[64,512,256]{2,1,0:T(8,128)}, s32[6,64]{1,0:T(8,128)S(1)}, f32[6,64,4,128]{3,1,0,2:T(8,128)S(1)}, s32[]{:T(128)}) while((s32[]{:T(128)}, f32[64,512,256]{2,1,0:T(8,128)}, s32[6,64]{1,0:T(8,128)S(1)}, f32[6,64,4,128]{3,1,0,2:T(8,128)S(1)}, s32[]{:T(128)}) %tuple.44), condition=%wide.region_11.12_spmd, body=%wide.region_9.11_spmd.sunk | while | flops 2193621760 | bytes 143267664 | solution.py:183
  73.8 3.9 multiply_convert_fusion.3
  77.7 13.1 fusion.196
  90.9 68.7 %scatter_fusion = f32[64,512,256]{2,1,0:T(8,128)} fusion(f32[64,512,256]{2,1,0:T(8,128)} %get-tuple-element.118, s32[64]{0:T(128)S(1)} %fusion.195, f32[64,512,256]{2,1,0:T(8,128)} %fusion.196), kind=kCustom, calls=%fused_computation.clone.1 | custom fusion | flops 8388608 | bytes 100663552 | tf_op jit(solution)/shard_map/while/body/eval_jaxpr/scatter-add | solution.py:180
  163.4 13.1 fusion.196
  176.6 67.8 %scatter_fusion = f32[64,512,256]{2,1,0:T(8,128)} fusion(f32[64,512,256]{2,1,0:T(8,128)} %get-tuple-element.118, s32[64]{0:T(128)S(1)} %fusion.195, f32[64,512,256]{2,1,0:T(8,128)} %fusion.196), kind=kCustom, calls=%fused_computation.clone.1 | custom fusion | flops 8388608 | bytes 100663552 | tf_op jit(solution)/shard_map/while/body/eval_jaxpr/scatter-add | solution.py:180
  248.3 13.1 fusion.196
  261.4 67.9 %scatter_fusion = f32[64,512,256]{2,1,0:T(8,128)} fusion(f32[64,512,256]{2,1,0:T(8,128)} %get-tuple-element.118, s32[64]{0:T(128)S(1)} %fusion.195, f32[64,512,256]{2,1,0:T(8,128)} %fusion.196), kind=kCustom, calls=%fused_computation.clone.1 | custom fusion | flops 8388608 | bytes 100663552 | tf_op jit(solution)/shard_map/while/body/eval_jaxpr/scatter-add | solution.py:180
  329.4 3.9 multiply_convert_fusion.3
  333.2 13.2 fusion.196
  346.4 68.8 %scatter_fusion = f32[64,512,256]{2,1,0:T(8,128)} fusion(f32[64,512,256]{2,1,0:T(8,128)} %get-tuple-element.118, s32[64]{0:T(128)S(1)} %fusion.195, f32[64,512,256]{2,1,0:T(8,128)} %fusion.196), kind=kCustom, calls=%fused_computation.clone.1 | custom fusion | flops 8388608 | bytes 100663552 | tf_op jit(solution)/shard_map/while/body/eval_jaxpr/scatter-add | solution.py:180
  415.2 3.9 multiply_convert_fusion.3
  419.1 13.1 fusion.196
  432.2 68.0 %scatter_fusion = f32[64,512,256]{2,1,0:T(8,128)} fusion(f32[64,512,256]{2,1,0:T(8,128)} %get-tuple-element.118, s32[64]{0:T(128)S(1)} %fusion.195, f32[64,512,256]{2,1,0:T(8,128)} %fusion.196), kind=kCustom, calls=%fused_computation.clone.1 | custom fusion | flops 8388608 | bytes 100663552 | tf_op jit(solution)/shard_map/while/body/eval_jaxpr/scatter-add | solution.py:180
  504.1 13.1 fusion.196
  517.3 67.5 %scatter_fusion = f32[64,512,256]{2,1,0:T(8,128)} fusion(f32[64,512,256]{2,1,0:T(8,128)} %get-tuple-element.118, s32[64]{0:T(128)S(1)} %fusion.195, f32[64,512,256]{2,1,0:T(8,128)} %fusion.196), kind=kCustom, calls=%fused_computation.clone.1 | custom fusion | flops 8388608 | bytes 100663552 | tf_op jit(solution)/shard_map/while/body/eval_jaxpr/scatter-add | solution.py:180
  584.8 31.8 %copy.102 = f32[64,512,256]{2,0,1:T(8,128)} copy(f32[64,512,256]{2,1,0:T(8,128)} %get-tuple-element.27) | data formatting | bytes 67108864 | tf_op jit(solution)/shard_map/while | solution.py:183
  616.6 21.9 %fusion.20 = f32[64,512,128]{2,0,1:T(8,128)} fusion(f32[64,512,256]{2,0,1:T(8,128)} %copy.102), kind=kOutput, calls=%fused_computation.36 | convolution fusion | flops 3221282816 | bytes 33554432 | tf_op jit(solution)/shard_map/nrq,kn->rkq/dot_general | solution.py:70
  638.5 22.1 %fusion.18 = f32[64,512,128]{2,0,1:T(8,128)} fusion(f32[64,512,256]{2,0,1:T(8,128)} %copy.102), kind=kOutput, calls=%fused_computation.34 | convolution fusion | flops 3221282816 | bytes 33554432 | tf_op jit(solution)/shard_map/nrq,kn->rkq/dot_general | solution.py:70
  660.6 24.3 %fusion.34 = f32[64,512,128]{2,0,1:T(8,128)} fusion(f32[64,512,128]{2,0,1:T(8,128)} %fusion.20, f32[64,512,256]{2,0,1:T(8,128)} %copy.102), kind=kOutput, calls=%fused_computation.50 | convolution fusion | flops 3225477120 | bytes 50331648 | tf_op jit(solution)/shard_map/nrq,kn->rkq/dot_general | solution.py:70
  684.9 33.1 %subtract_bitcast_fusion = (f32[512,64,128]{2,1,0:T(8,128)}, f32[512,64,128]{2,1,0:T(8,128)}) fusion(f32[64,512,128]{2,0,1:T(8,128)} %fusion.34, f32[64,128]{1,0:T(8,128)S(1)} %copy-done.2, f32[64,128]{1,0:T(8,128)S(1)} %copy-done.3, f32[64,512,128]{2,0,1:T(8,128)} %fusion.18, f32[64,512,256]{2,0,1:T(8,128)} %copy.102), kind=kOutput, calls=%fused_computation.33 | convolution fusion | flops 3250642944 | bytes 83951616 | tf_op jit(solution)/shard_map/nrq,kn->rkq/dot_general | solution.py:70
  718.0 34.3 %fusion.26 = f32[64,512,64]{1,0,2:T(8,128)S(1)} fusion(f32[512,64,128]{2,1,0:T(8,128)} %get-tuple-element.65, s32[64]{0:T(128)S(1)} %copy-done.4), kind=kOutput, calls=%fused_computation.42 | convolution fusion | flops 3221340160 | bytes 25166080 | tf_op jit(solution)/shard_map/rkq,qj->rjk/dot_general | solution.py:70
  752.3 33.9 %add_bitcast_fusion.1 = f32[512,64,64]{0,1,2:T(8,128)} fusion(f32[64,512,64]{1,0,2:T(8,128)S(1)} %fusion.26, f32[512,64,128]{2,1,0:T(8,128)} %get-tuple-element.64, s32[64]{0:T(128)S(1)} %copy-done.4), kind=kOutput, calls=%fused_computation.58 | convolution fusion | flops 3223437312 | bytes 33554688 | tf_op jit(solution)/shard_map/rkq,qj->rjk/dot_general | solution.py:70
  786.2 11.5 copy.111
  797.6 23.3 %all-to-all-start.3 = ((f32[512,16,256]{0,2,1:T(8,128)}), f32[512,16,256]{0,2,1:T(8,128)}, u32[]{:S(2)}, u32[]{:S(2)}) async-start(f32[512,16,256]{0,2,1:T(8,128)} %bitcast.113), calls=%async_computation.4 | async-start | bytes 16777216 | tf_op jit(solution)/shard_map/all_to_all | solution.py:201
  821.0 34.5 %fusion.28 = f32[64,512,64]{1,0,2:T(8,128)S(1)} fusion(f32[512,64,128]{2,1,0:T(8,128)} %get-tuple-element.65, s32[64]{0:T(128)S(1)} %copy-done.4), kind=kOutput, calls=%fused_computation.44 | convolution fusion | flops 3221340160 | bytes 25166080 | tf_op jit(solution)/shard_map/rkq,qj->rjk/dot_general | solution.py:70
  855.5 34.5 %subtract_bitcast_fusion.1 = f32[512,64,64]{0,1,2:T(8,128)} fusion(f32[64,512,64]{1,0,2:T(8,128)S(1)} %fusion.28, f32[512,64,128]{2,1,0:T(8,128)} %get-tuple-element.64, s32[64]{0:T(128)S(1)} %copy-done.4), kind=kOutput, calls=%fused_computation.59 | convolution fusion | flops 3223437312 | bytes 33554688 | tf_op jit(solution)/shard_map/rkq,qj->rjk/dot_general | solution.py:70
  890.0 11.4 copy.106
  901.5 103.4 %all-to-all-done.3 = f32[512,16,256]{0,2,1:T(8,128)} async-done(((f32[512,16,256]{0,2,1:T(8,128)}), f32[512,16,256]{0,2,1:T(8,128)}, u32[]{:S(2)}, u32[]{:S(2)}) %all-to-all-start.3) | async-done | bytes 8388640 | tf_op jit(solution)/shard_map/all_to_all | solution.py:201
  1004.9 5.1 all-to-all-start.2
  1010.2 9.3 copy.112
  1019.5 17.7 %fusion.44 = f32[64,128,256]{2,0,1:T(8,128)} fusion(f32[64,128,256]{2,1,0:T(8,128)} %bitcast.108), kind=kOutput, calls=%fused_computation.60 | convolution fusion | flops 1610670080 | bytes 16777216 | tf_op jit(solution)/shard_map/anqb,kn->akqb/dot_general | solution.py:70
  1037.2 13.2 fusion.46
  1050.4 146.4 %all-to-all-done.2 = f32[512,16,256]{0,2,1:T(8,128)} async-done(((f32[512,16,256]{0,2,1:T(8,128)}), f32[512,16,256]{0,2,1:T(8,128)}, u32[]{:S(2)}, u32[]{:S(2)}) %all-to-all-start.2) | async-done | bytes 8388640 | tf_op jit(solution)/shard_map/all_to_all | solution.py:200
  1196.7 9.2 copy.107
  1206.0 17.8 %fusion.50 = f32[64,128,256]{2,0,1:T(8,128)} fusion(f32[64,128,256]{2,1,0:T(8,128)} %bitcast.110), kind=kOutput, calls=%fused_computation.66 | convolution fusion | flops 1610670080 | bytes 16777216 | tf_op jit(solution)/shard_map/anqb,kn->akqb/dot_general | solution.py:70
  1223.8 19.4 %multiply_subtract_fusion = (f32[64,128,256]{2,0,1:T(8,128)S(1)}, f32[64,128,256]{2,0,1:T(8,128)}) fusion(f32[64,128]{0,1:T(8,128)S(1)} %copy.117, f32[64,128]{0,1:T(8,128)S(1)} %copy.114, f32[64,128,256]{2,0,1:T(8,128)} %fusion.44, f32[64,128,256]{2,0,1:T(8,128)} %fusion.50, f32[64,128,256]{2,0,1:T(8,128)} %fusion.46, f32[64,128,256]{2,1,0:T(8,128)S(1)} %bitcast.111), kind=kOutput, calls=%fused_computation.57 | convolution fusion | flops 1627447296 | bytes 50397184 | tf_op jit(solution)/shard_map/anqb,kn->akqb/dot_general | solution.py:70
  1243.2 13.5 fusion.40
  1256.7 10.4 fusion.63
  1272.6 97.3 %all_to_all.59 = f32[16,256,256]{2,1,0:T(8,128)} all-to-all(f32[16,256,256]{2,1,0:T(8,128)S(1)} %fusion.57), channel_id=1, replica_groups=mesh['tm'=2,'uv'=16] {'uv'}, dimensions={0} | all-to-all | bytes 8388608 | tf_op jit(solution)/shard_map/all_to_all | solution.py:205
  1369.9 5.3 copy.121
  1375.2 5.6 copy.122
  (84 shorter events, 33.3 us)
Async XLA Ops:
  6.5 25.0 %copy-start.5 = (s32[1,128]{1,0:T(1,128)S(1)}, s32[1,128]{1,0:T(1,128)}, u32[]{:S(2)}) copy-start(s32[1,128]{1,0:T(1,128)} %param.14) | copy-start | bytes 1540
  6.5 24.0 %reduce-scatter.2.cloned.1.call-start = ((), (), s32[]{:S(2)}) async-start(), calls=%async_computation.6 | async-start | bytes 786432 | tf_op jit(solution)/shard_map/reduce_scatter | solution.py:137
  19.1 18.3 %all-to-all-start = ((s32[16,1,24]{2,1,0:T(1,128)}), s32[16,1,24]{2,1,0:T(1,128)S(1)}, u32[]{:S(2)}, u32[]{:S(2)}) async-start(s32[16,1,24]{2,1,0:T(1,128)} %all_to_all.43), calls=%async_computation | async-start | bytes 16384 | tf_op jit(solution)/shard_map/all_to_all | solution.py:170
  37.4 25.3 %all-to-all-start.1 = ((f32[16,24,4,128]{3,1,2,0:T(8,128)}), f32[16,24,4,128]{3,1,2,0:T(8,128)S(1)}, u32[]{:S(2)}, u32[]{:S(2)}) async-start(f32[16,24,4,128]{3,1,2,0:T(8,128)} %copy.99), calls=%async_computation.2 | async-start | bytes 1572864 | tf_op jit(solution)/shard_map/all_to_all | solution.py:163
  660.6 24.3 %copy-start.2 = (f32[64,128]{1,0:T(8,128)S(1)}, f32[64,128]{1,0:T(8,128)}, u32[]{:S(2)}) copy-start(f32[64,128]{1,0:T(8,128)} %get-tuple-element.73) | copy-start | bytes 98308
  660.6 24.3 %copy-start.3 = (f32[64,128]{1,0:T(8,128)S(1)}, f32[64,128]{1,0:T(8,128)}, u32[]{:S(2)}) copy-start(f32[64,128]{1,0:T(8,128)} %get-tuple-element.74) | copy-start | bytes 98308
  684.9 33.1 %copy-start.4 = (s32[64]{0:T(128)S(1)}, s32[64]{0:T(128)}, u32[]{:S(2)}) copy-start(s32[64]{0:T(128)} %pad_add_fusion) | copy-start | bytes 772
  797.6 207.2 %all-to-all-start.3 = ((f32[512,16,256]{0,2,1:T(8,128)}), f32[512,16,256]{0,2,1:T(8,128)}, u32[]{:S(2)}, u32[]{:S(2)}) async-start(f32[512,16,256]{0,2,1:T(8,128)} %bitcast.113), calls=%async_computation.4 | async-start | bytes 16777216 | tf_op jit(solution)/shard_map/all_to_all | solution.py:201
  1004.9 191.9 %all-to-all-start.2 = ((f32[512,16,256]{0,2,1:T(8,128)}), f32[512,16,256]{0,2,1:T(8,128)}, u32[]{:S(2)}, u32[]{:S(2)}) async-start(f32[512,16,256]{0,2,1:T(8,128)} %bitcast.112), calls=%async_computation.3 | async-start | bytes 16777216 | tf_op jit(solution)/shard_map/all_to_all | solution.py:200
  1019.5 17.7 %copy-start = (f32[16,512,256]{2,1,0:T(8,128)S(1)}, f32[16,512,256]{2,1,0:T(8,128)}, u32[]{:S(2)}) copy-start(f32[16,512,256]{2,1,0:T(8,128)} %copy.112) | copy-start | bytes 25165828
  1206.0 17.8 %copy-start.1 = (f32[16,512,256]{2,1,0:T(8,128)S(1)}, f32[16,512,256]{2,1,0:T(8,128)}, u32[]{:S(2)}) copy-start(f32[16,512,256]{2,1,0:T(8,128)} %copy.107) | copy-start | bytes 25165828
Sparse Core Ops, SparseCore 0:
  15.0 9.2 reduce-scatter.1
where the time goes:
time: 1400 us; the launch traced here: 1390 us
  other arithmetic  448 us (32%)
  matrix products  410 us (29%)
  waiting for transfers between devices  265 us (19%)
  local copies, waits for them, and re-layouts  110 us (8%)
  blocking collectives  97.3 us (7%)
  starting transfers between devices  42.8 us (3%)
  between operations  15.2 us (1%)
    scatter-add x6, other arithmetic, accumulate(): running.at[tile_group].add(grid_tiles(message_group, band_rows))  409 us
    dot_general x14, matrix products, mixed(): jnp.einsum(subscripts, values, weights, precision=lax.Precision.HIGHEST)  331 us
    all_to_all x1, waiting for transfers between devices, body(): lax.all_to_all(half_real, 'uv', split_axis=1, concat_axis=0, tiled=True)  146 us
    all_to_all x1, waiting for transfers between devices, body(): lax.all_to_all(half_imag, 'uv', split_axis=1, concat_axis=0, tiled=True)  103 us
    all_to_all x1, blocking collectives, body(): lax.all_to_all(finished, 'uv', split_axis=0, concat_axis=1, tiled=True)  97.3 us
    dot_general x6, matrix products, grid_tiles(): jnp.einsum('grj,gri->gji', left, right, preferred_element_type=jnp.float32)  78.9 us
    while x1, local copies, waits for them, and re-layouts, body(): lax.scan(accumulate, uv_grid, (received.reshape(-1, group_size, 4, VISIBI...  31.8 us
  transfers between devices with their start and end apart: 5, of which 3 were waited for; matrix products, arithmetic and copies ran while one was open for 10% of the time, Pallas kernels for 0%

commit v1 on v0

v1 whole, which is shorter than its diff:
```python
import functools
import math

import jax
import jax.numpy as jnp
import numpy as np
from jax import lax
from jax.experimental import pallas as pl
from jax.experimental.pallas import tpu as pltpu
from jax.sharding import PartitionSpec as P

NG = 8192
TILE = 128
VISIBILITY_ROWS = 128
SUBS = 16
NBIN = 8
BL_DEV = 2048
NI = 4096


kernel_width = 1.3
ramp_width = 0.25


def kurtosis_weight(first_sum, second, window):
    ratio = SUBS * second / (first_sum * first_sum)
    kurtosis = (SUBS + 1.0) / (SUBS - 1.0) * (ratio - 1.0)
    lower = window[0].astype(jnp.float32) / 1000.0
    upper = window[1].astype(jnp.float32) / 1000.0
    return jnp.clip((kurtosis - lower) / ramp_width, 0.0, 1.0) * jnp.clip(
        (upper - kurtosis) / ramp_width, 0.0, 1.0
    )


HALF = NG // 2
PAD = 16


def spread(gap):
    return jnp.exp(gap * gap * (-0.5 / (kernel_width * kernel_width)))


def grid_kernel(band, codes, first, spots, values, out, edge, picked):
    blocks = spots.shape[0]
    width = out.shape[2]
    base_w = first[0]
    step = 256

    def clear(at, carry):
        rows = pl.ds(pl.multiple_of(at * step, step), step)
        out[0, rows, :] = jnp.zeros((step, width), jnp.float32)
        out[1, rows, :] = jnp.zeros((step, width), jnp.float32)
        edge[rows, :] = jnp.zeros((step, TILE), jnp.float32)
        return carry

    lax.fori_loop(0, NG // step, clear, 0)

    def reach(tile):
        low = jnp.where(tile * TILE >= HALF, tile * TILE - HALF, HALF - tile * TILE - (TILE - 1))
        return low, (low < base_w + width) & (low + TILE > base_w)

    def pick(at, count):
        tile = lax.rem(codes[at], NG // TILE)
        _, mine = reach(tile)
        picked[count] = at
        return count + jnp.where(mine | (tile == 0), 1, 0)

    count = lax.fori_loop(0, blocks, pick, 0, unroll=8)
    tall = band + PAD
    p_ids = lax.broadcasted_iota(jnp.int32, (tall, VISIBILITY_ROWS), 0)
    w_ids = lax.broadcasted_iota(jnp.int32, (width, VISIBILITY_ROWS), 0)
    e_ids = lax.broadcasted_iota(jnp.int32, (TILE, VISIBILITY_ROWS), 0)

    def product(left, right):
        return lax.dot_general(
            left, right, (((1,), (1,)), ((), ())), preferred_element_type=jnp.float32
        )

    def add(at, carry):
        block = picked[at]
        code = codes[block]
        owner = lax.div(code, NG // TILE)
        tile = lax.rem(code, NG // TILE)
        low, mine = reach(tile)
        mirrored = tile * TILE < HALF
        sign = jnp.where(mirrored, -1, 1)
        eight = pl.ds(pl.multiple_of(lax.div(block, 8) * 8, 8), 8)
        here = lax.broadcasted_iota(jnp.int32, (8, 2 * TILE), 0) == lax.rem(block, 8)
        spot = jnp.sum(jnp.where(here, spots[eight, :], 0.0), axis=0, keepdims=True)
        value_row = jnp.sum(jnp.where(here, values[eight, :], 0.0), axis=0, keepdims=True)
        u, v = spot[:, :TILE], spot[:, TILE:]
        real, imag = value_row[:, :TILE], value_row[:, TILE:] * sign.astype(jnp.float32)
        j_ids = sign * p_ids + jnp.where(mirrored, band, 0)
        left = jnp.where(
            (j_ids >= 0) & (j_ids < band), spread(j_ids.astype(jnp.float32) - v), 0.0
        ).astype(jnp.bfloat16)
        start = jnp.where(mirrored, NG - band * (owner + 1), band * owner)
        main_rows = pl.ds(pl.multiple_of(start, band), band)
        last_rows = pl.ds(pl.multiple_of(lax.rem(start + band, NG), band), PAD)

        @pl.when(mine)
        def _():
            i_ids = sign * (w_ids + base_w - low) + jnp.where(mirrored, TILE - 1, 0)
            across = jnp.where(
                (i_ids >= 0) & (i_ids < TILE), spread(i_ids.astype(jnp.float32) - u), 0.0
            )
            for part, value in ((0, real), (1, imag)):
                made = product(left, (value * across).astype(jnp.bfloat16))
                out[part, main_rows, :] += made[:band]
                out[part, last_rows, :] += made[band:]

        @pl.when(tile == 0)
        def _():
            across = spread(u)
            right = jnp.where(
                e_ids == 0, real * across, jnp.where(e_ids == 1, imag * across, 0.0)
            ).astype(jnp.bfloat16)
            made = product(left, right)
            edge[main_rows, :] += made[:band]
            edge[last_rows, :] += made[band:]

        return carry

    lax.fori_loop(0, count, add, 0)


def grid_blocks(codes, first, spots, values, band, width):
    vmem = pl.BlockSpec(memory_space=pltpu.VMEM)
    smem = pl.BlockSpec(memory_space=pltpu.SMEM)
    return pl.pallas_call(
        functools.partial(grid_kernel, band),
        out_shape=(
            jax.ShapeDtypeStruct((2, NG, width), jnp.float32),
            jax.ShapeDtypeStruct((NG, TILE), jnp.float32),
        ),
        in_specs=[smem, smem, vmem, vmem],
        out_specs=(vmem, vmem),
        scratch_shapes=[pltpu.SMEM((spots.shape[0] + 8,), jnp.int32)],
        compiler_params=pltpu.CompilerParams(vmem_limit_bytes=56 * 1024 * 1024),
    )(codes, first, spots, values)


def taper(indices):
    offset = indices.astype(jnp.float32) - NI // 2
    scaled = offset / NG
    return jnp.exp(-2.0 * math.pi * math.pi * kernel_width * kernel_width * scaled * scaled)


def rotation(product, modulus):
    angles = (product % modulus) * (2.0 * math.pi / modulus)
    cos_part, sin_part = np.cos(angles), np.sin(angles)
    return np.stack(
        [np.stack([cos_part, sin_part], -1), np.stack([-sin_part, cos_part], -1)], -2
    ).astype(np.float32)


def transform_tables(inner, count):
    outer = NG // inner
    kept = NI // outer
    j_ids = np.arange(kept) - kept // 2
    k_ids = np.arange(outer)
    q_ids = np.arange(inner)
    one = rotation(np.arange(count)[:, None] * k_ids[None, :], outer)
    two = rotation(
        q_ids[None, :, None] * (k_ids[:, None, None] + outer * j_ids[None, None, :]), NG
    )
    return one, two


mix = functools.partial(
    jnp.einsum, precision=lax.Precision.HIGH, preferred_element_type=jnp.float32
)


def body(visibilities, u_offset, v_offset, block_owner, block_u_tile, block_count, sk_window):
    owners = lax.axis_size("uv")
    local_bin_count = visibilities.shape[0]
    antenna_pairs = visibilities.shape[4]
    local_block_count = local_bin_count * antenna_pairs // VISIBILITY_ROWS
    blocked = (local_block_count, VISIBILITY_ROWS)
    spots = lax.all_gather(
        jnp.concatenate([u_offset[0].reshape(blocked), v_offset[0].reshape(blocked)], axis=1),
        "uv",
        tiled=True,
    )
    codes = lax.all_gather(
        block_owner[0, :, 0] * (NG // TILE) + block_u_tile[0], "uv", tiled=True
    )
    real_part = visibilities[:, :, :, 0].astype(jnp.float32)
    imag_part = visibilities[:, :, :, 1].astype(jnp.float32)
    powers = real_part * real_part + imag_part * imag_part
    local_sums = jnp.stack(
        [
            jnp.sum(real_part, axis=1),
            jnp.sum(imag_part, axis=1),
            jnp.sum(powers, axis=1),
            jnp.sum(powers * powers, axis=1),
        ],
        axis=0,
    )
    local_sums = local_sums.transpose(2, 0, 1, 3)
    totals = lax.psum_scatter(local_sums, "tm", scatter_dimension=0, tiled=True)[0]
    weight = kurtosis_weight(totals[2], totals[3], sk_window[0])
    avg_real = (weight * totals[0] / SUBS).reshape(blocked)
    avg_imag = (weight * totals[1] / SUBS).reshape(blocked)
    live_rows = jnp.arange(VISIBILITY_ROWS)[None, :] < block_count[0][:, None]
    avg_real = jnp.where(live_rows, avg_real, 0.0)
    avg_imag = jnp.where(live_rows, avg_imag, 0.0)
    values = lax.all_gather(
        jnp.concatenate([avg_real, avg_imag], axis=1), "uv", tiled=True
    )
    band = NG // owners
    width = HALF // owners
    me = lax.axis_index("uv")
    uv_grid, edge = grid_blocks(
        codes, (me * width)[None].astype(jnp.int32), spots, values, band, width
    )

    outer = NG // TILE
    one, two = transform_tables(TILE, outer)
    rows_mine = NI // owners
    jj_mine = rows_mine // outer
    stage = mix("cnqw,nkcd->dkqw", uv_grid.reshape(2, outer, TILE, width), one)
    two_split = two.reshape(outer, TILE, owners, jj_mine, 2, 2)

    edge_in = edge[:, :2].T.reshape(2, outer, TILE)
    edge_stage = mix("cnq,nkcd->dkq", edge_in, one)
    edge_all = mix("ckq,kqjc->jk", edge_stage, two[..., 0])
    edge_mine = lax.dynamic_slice_in_dim(edge_all, me * jj_mine, jj_mine, 0).reshape(rows_mine)

    inner = min(width, TILE)
    per_owner = width // inner
    outer_l = NG // inner
    row_one, row_two = transform_tables(inner, HALF // inner)
    row_one = row_one.reshape(owners, per_owner, outer_l, 2, 2)
    row_two = row_two[..., 0]
    scale = 1.0 / math.sqrt(NBIN * BL_DEV * owners)
    col_ids = jnp.arange(NI)
    parts = 2 if jj_mine % 2 == 0 else 1
    jj_part = jj_mine // parts
    rows_part = rows_mine // parts
    images = []
    for part in range(parts):
        table = two_split[:, :, :, part * jj_part : (part + 1) * jj_part]
        columns = mix("ckqw,kqejcd->edjkw", stage, table)
        columns = columns.reshape(owners, 2, rows_part, per_owner, inner).transpose(0, 1, 3, 2, 4)
        columns = lax.all_to_all(columns, "uv", split_axis=0, concat_axis=0, tiled=True)
        row_stage = mix("scnmq,snkcd->dkmq", columns, row_one)
        image = mix("ckmq,kqjc->mjk", row_stage, row_two).reshape(rows_part, NI)
        row_ids = me * rows_mine + part * rows_part + jnp.arange(rows_part)
        edge_part = edge_mine[part * rows_part : (part + 1) * rows_part]
        col_sign = 1.0 - 2.0 * (col_ids % 2).astype(jnp.float32)
        row_sign = 1.0 - 2.0 * (row_ids % 2).astype(jnp.float32)
        image = image + edge_part[:, None] * col_sign[None, :]
        row_factor = row_sign * scale / taper(row_ids)
        images.append(image * row_factor[:, None] / taper(col_ids)[None, :])
    return jnp.concatenate(images, axis=0)[None]


def solution(mesh):
    placed = (
        P(None, "tm", None, None, "uv"),
        P("tm", None, "uv"),
        P("tm", None, "uv"),
        P("tm", "uv", None),
        P("tm", "uv"),
        P("tm", "uv"),
        P("tm", None),
    )
    return jax.shard_map(
        body, mesh=mesh, in_specs=placed, out_specs=P("tm", "uv", None), check_vma=False
    )
```

time: 1400 us -> 578 us (0.41)
  other arithmetic: 448 us -> 13.6 us
  matrix products: 410 us -> 106 us
  Pallas kernels: 0 us -> 107 us
  blocking collectives: 97.3 us -> 29.1 us
  local copies, waits for them, and re-layouts: 110 us -> 44.8 us
  waiting for transfers between devices: 265 us -> 220 us
    scatter-add x6 -> x0, other arithmetic: 409 us -> none  [accumulate(): running.at[tile_group].add(grid_tiles(message_group, band_rows))]
    dot_general x20 -> x9, matrix products: 410 us -> 106 us  [the longest x2 42 us: body(): columns = mix('ckqw,kqejcd->edjkw', stage, table)]
    all_to_all x4 -> x2, waiting for transfers between devices: 265 us -> 127 us  [body(): lax.all_to_all(columns, 'uv', split_axis=0, concat_axis=0, tiled=True)]
    pallas_call x0 -> x1, Pallas kernels: none -> 107 us  [grid_blocks(): pl.pallas_call(functools.partial(grid_kernel, band), out_shape=(jax.Shape...]
    all_to_all x1 -> x0, blocking collectives: 97.3 us -> none  [body(): lax.all_to_all(finished, 'uv', split_axis=0, concat_axis=1, tiled=True)]
    all_gather x0 -> x2, waiting for transfers between devices: none -> 86.2 us  [the longest x1 62.5 us: body(): lax.all_gather(jnp.concatenate([avg_real, avg_imag], axis=1), 'uv', tiled...]
    while x1 -> x0, local copies, waits for them, and re-layouts: 31.8 us -> none  [body(): lax.scan(accumulate, uv_grid, (received.reshape(-1, group_size, 4, VISIBI...]
    all_gather x0 -> x1, blocking collectives: none -> 29.1 us  [body(): lax.all_gather(block_owner[0, :, 0] * (NG // TILE) + block_u_tile[0], 'uv...]
  transfers between devices with their start and end apart: 5 -> 5, of which waited for: 3 -> 5; matrix products, arithmetic and copies ran while one was open for 10% -> 12% of each run, Pallas kernels for 0% -> 0%
where the time goes in v1:
time: 578 us; the launch traced here: 574 us
  waiting for transfers between devices  220 us (38%)
  Pallas kernels  107 us (19%)
  matrix products  106 us (18%)
  local copies, waits for them, and re-layouts  44.8 us (8%)
  starting transfers between devices  36.5 us (6%)
  blocking collectives  29.1 us (5%)
  between operations  16.9 us (3%)
  other arithmetic  13.6 us (2%)
    all_to_all x2, waiting for transfers between devices, body(): lax.all_to_all(columns, 'uv', split_axis=0, concat_axis=0, tiled=True)  127 us
    pallas_call x1, Pallas kernels, grid_blocks(): pl.pallas_call(functools.partial(grid_kernel, band), out_shape=(jax.Shape...  107 us
    all_gather x1, waiting for transfers between devices, body(): lax.all_gather(jnp.concatenate([avg_real, avg_imag], axis=1), 'uv', tiled...  62.5 us
    dot_general x2, matrix products, body(): columns = mix('ckqw,kqejcd->edjkw', stage, table)  42 us
    all_to_all x2, starting transfers between devices, body(): lax.all_to_all(columns, 'uv', split_axis=0, concat_axis=0, tiled=True)  36.4 us
    all_gather x1, blocking collectives, body(): lax.all_gather(block_owner[0, :, 0] * (NG // TILE) + block_u_tile[0], 'uv...  29.1 us
    dot_general x1, matrix products, body(): stage = mix('cnqw,nkcd->dkqw', uv_grid.reshape(2, outer, TILE, width), one)  25.7 us
    all_gather x1, waiting for transfers between devices, body(): lax.all_gather(jnp.concatenate([u_offset[0].reshape(blocked), v_offset[0]...  23.7 us
  transfers between devices with their start and end apart: 5, of which 5 were waited for; matrix products, arithmetic and copies ran while one was open for 12% of the time, Pallas kernels for 0%

profile of v1, /device:TPU:14, one launch (start us, length us, event | category | flops | bytes accessed | tf_op | source)
XLA Modules:
  0.0 574.2 jit_solution(3523917315142776950)
XLA Ops:
  7.4 0.0 reduce-scatter.2.cloned.1.call-start
  7.4 5.1 convert_reduce_fusion.1
  12.6 1.9 fusion.68
  14.5 0.3 maximum_bitcast_fusion.1
  14.7 1.1 copy.41
  15.8 0.0 reduce-scatter.2.cloned.1.call-update
  15.8 0.0 all-gather.4.cloned.1.call-start
  16.0 0.7 pad_maximum_fusion
  16.6 0.0 all-gather.4.cloned.1.call-update
  16.7 0.0 all-gather.6.cloned.1.call-start
  16.7 0.6 fusion.70
  18.7 6.6 %reduce-scatter.2.cloned.1.call-done = f32[1,4,8,2048]{3,2,1,0:T(8,128)} async-done(((f32[2,4,8,2048]{3,2,1,0:T(8,128)}), f32[1,4,8,2048]{3,2,1,0:T(8,128)}) %reduce-scatter.2.cloned.1.call-update) | async-done | bytes 262160 | tf_op jit(solution)/shard_map/reduce_scatter | solution.py:202
  25.3 1.0 fusion.40
  26.3 0.1 fusion.46
  26.4 0.7 pad_maximum_fusion.1
  27.1 0.0 all-gather.6.cloned.1.call-update
  27.2 29.1 %all-gather = s32[16,1,128]{2,1,0:T(1,128)} all-gather(s32[1,1,128]{2,1,0:T(1,128)S(1)} %fusion.67), channel_id=1, replica_groups=mesh['tm'=2,'uv'=16] {'uv'}, dimensions={0}, use_global_device_ids=true | all-gather | bytes 8704 | tf_op jit(solution)/shard_map/all_gather | solution.py:186
  56.2 23.7 %all-gather.4.cloned.1.call-done.spots = f32[2048,256]{1,0:T(8,128)} async-done(((f32[128,256]{1,0:T(8,128)}), f32[2048,256]{1,0:T(8,128)}) %all-gather.4.cloned.1.call-update) | async-done | bytes 2097168 | tf_op jit(solution)/shard_map/all_gather | solution.py:181
  79.9 62.5 %all-gather.6.cloned.1.call-done.values = f32[2048,256]{1,0:T(8,128)} async-done(((f32[128,256]{1,0:T(8,128)}), f32[2048,256]{1,0:T(8,128)}) %all-gather.6.cloned.1.call-update) | async-done | bytes 2097168 | tf_op jit(solution)/shard_map/all_gather | solution.py:209
  142.5 107.3 %shard_map.154 = (f32[2,8192,256]{2,1,0:T(8,128)}, f32[8192,128]{1,0:T(8,128)}) custom-call(s32[2048]{0:T(1024)} %bitcast.125, s32[1]{0:T(128)} %bitcast.4.first, f32[2048,256]{1,0:T(8,128)} %all-gather.4.cloned.1.call-done.spots, f32[2048,256]{1,0:T(8,128)} %all-gather.6.cloned.1.call-done.values), custom_call_target="tpu_custom_call" | custom-call | tf_op jit(solution)/shard_map/pallas_call | solution.py:130
  249.7 25.7 %fusion.6 = f32[2,64,128,256,1,1]{3,1,0,2,5,4:T(8,128)} fusion(f32[64,64,2,2,1]{0,1,2,3,4:T(8,128)S(1)} %copy-done.4, f32[2,64,128,256,1]{3,2,1,0,4:T(8,128)} %bitcast.116), kind=kOutput, calls=%fused_computation.6 | convolution fusion | flops 3221225472 | bytes 33619968 | tf_op jit(solution)/shard_map/cnqw,nkcd->dkqw/dot_general | solution.py:223
  275.5 20.3 %fusion.23 = f32[16,2,2,64,256]{4,0,1,2,3:T(8,128)S(1)} fusion(f32[64,128,16,2,2,2]{1,2,4,5,3,0:T(8,128)S(1)} %copy-done.2, f32[2,64,128,256,1,1]{3,1,0,2,5,4:T(8,128)} %fusion.6), kind=kOutput, calls=%fused_computation.18 | convolution fusion | flops 1610612736 | bytes 25165824 | tf_op jit(solution)/shard_map/ckqw,kqejcd->edjkw/dot_general | solution.py:245
  295.8 4.4 copy.44
  300.2 5.8 %reshape.142 = f32[16,2,128,2,128]{4,3,2,1,0:T(2,128)} reshape(f32[16,2,2,64,256]{4,3,2,1,0:T(8,128)} %copy.44) | data formatting | bytes 8388608 | tf_op jit(solution)/shard_map/reshape | solution.py:246
  306.0 5.6 copy.45
  311.7 31.0 %all-to-all-start = ((f32[16,2,2,128,128]{4,2,1,3,0:T(2,128)}), f32[16,2,2,128,128]{4,2,1,3,0:T(2,128)}, u32[]{:S(2)}, u32[]{:S(2)}) async-start(f32[16,2,2,128,128]{4,2,1,3,0:T(2,128)} %copy.45), calls=%async_computation.1 | async-start | bytes 8388608 | tf_op jit(solution)/shard_map/all_to_all | solution.py:247
  342.6 21.7 %fusion.26 = f32[16,2,2,64,256]{4,0,1,2,3:T(8,128)S(1)} fusion(f32[64,128,16,2,2,2]{1,2,4,5,3,0:T(8,128)} %constant.109.clone, f32[2,64,128,256,1,1]{3,1,0,2,5,4:T(8,128)} %fusion.6), kind=kOutput, calls=%fused_computation.19 | convolution fusion | flops 1610612736 | bytes 25165824 | tf_op jit(solution)/shard_map/ckqw,kqejcd->edjkw/dot_general | solution.py:245
  364.3 4.4 copy.51
  368.7 6.0 %reshape.145 = f32[16,2,128,2,128]{4,3,2,1,0:T(2,128)} reshape(f32[16,2,2,64,256]{4,3,2,1,0:T(8,128)} %copy.51) | data formatting | bytes 8388608 | tf_op jit(solution)/shard_map/reshape | solution.py:246
  374.7 5.6 copy.52
  380.3 56.1 %all-to-all-done = f32[16,2,2,128,128]{4,2,1,3,0:T(2,128)} async-done(((f32[16,2,2,128,128]{4,2,1,3,0:T(2,128)}), f32[16,2,2,128,128]{4,2,1,3,0:T(2,128)}, u32[]{:S(2)}, u32[]{:S(2)}) %all-to-all-start) | async-done | bytes 4194336 | tf_op jit(solution)/shard_map/all_to_all | solution.py:247
  436.4 5.4 all-to-all-start.1
  441.9 2.9 copy.49
  444.7 0.2 convolution_bitcast_fusion
  445.0 3.9 fusion.47
  448.9 0.1 copy.66
  449.0 0.1 mul.217
  449.1 0.1 mul.232
  449.2 8.4 %fusion.17 = f32[2,64,128,128]{3,1,0,2:T(8,128)S(1)} fusion(f32[16,2,64,2,2,1]{2,0,1,3,4,5:T(8,128)S(1)} %copy-done.3, f32[16,2,2,128,128,1]{4,2,1,3,0,5:T(2,128)} %bitcast.24), kind=kOutput, calls=%fused_computation.16 | convolution fusion | flops 805306368 | bytes 12615680 | tf_op jit(solution)/shard_map/scnmq,snkcd->dkmq/dot_general | solution.py:248
  457.6 8.8 %fusion.33 = f32[128,64,64]{0,1,2:T(8,128)S(1)} fusion(f32[64,128,64,2]{1,2,3,0:T(8,128)S(1)} %copy-done, f32[2,64,128,128]{3,1,0,2:T(8,128)S(1)} %fusion.17), kind=kOutput, calls=%fused_computation.26 | convolution fusion | flops 805306368 | bytes 14680064 | tf_op jit(solution)/shard_map/ckmq,kqjc->mjk/dot_general | solution.py:249
  466.3 1.2 copy.48
  467.6 70.9 %all-to-all-done.1 = f32[16,2,2,128,128]{4,2,1,3,0:T(2,128)} async-done(((f32[16,2,2,128,128]{4,2,1,3,0:T(2,128)}), f32[16,2,2,128,128]{4,2,1,3,0:T(2,128)}, u32[]{:S(2)}, u32[]{:S(2)}) %all-to-all-start.1) | async-done | bytes 4194336 | tf_op jit(solution)/shard_map/all_to_all | solution.py:247
  538.4 8.4 %fusion.20 = f32[2,64,128,128]{3,1,0,2:T(8,128)S(1)} fusion(f32[16,2,64,2,2,1]{2,0,1,3,4,5:T(8,128)S(1)} %copy-done.3, f32[16,2,2,128,128,1]{4,2,1,3,0,5:T(2,128)} %bitcast.48), kind=kOutput, calls=%fused_computation.17 | convolution fusion | flops 805306368 | bytes 12615680 | tf_op jit(solution)/shard_map/scnmq,snkcd->dkmq/dot_general | solution.py:248
  546.8 8.8 %fusion.36 = f32[128,64,64]{0,1,2:T(8,128)S(1)} fusion(f32[64,128,64,2]{1,2,3,0:T(8,128)S(1)} %copy-done.1, f32[2,64,128,128]{3,1,0,2:T(8,128)S(1)} %fusion.20), kind=kOutput, calls=%fused_computation.27 | convolution fusion | flops 805306368 | bytes 14680064 | tf_op jit(solution)/shard_map/ckmq,kqjc->mjk/dot_general | solution.py:249
  555.6 1.2 copy.55
  556.8 1.7 fusion.32
  558.6 2.2 maximum_bitcast_fusion
  560.8 5.6 copy.56
  (33 shorter events, 0.2 us)
Async XLA Ops:
  7.4 8.5 %copy-start.6 = (f32[1,8,2048]{2,1,0:T(8,128)S(1)}, f32[1,8,2048]{2,1,0:T(8,128)}, u32[]{:S(2)}) copy-start(f32[1,8,2048]{2,1,0:T(8,128)} %param.17) | copy-start | bytes 196612
  7.4 8.6 %copy-start.7 = (f32[1,8,2048]{2,1,0:T(8,128)S(1)}, f32[1,8,2048]{2,1,0:T(8,128)}, u32[]{:S(2)}) copy-start(f32[1,8,2048]{2,1,0:T(8,128)} %param.18) | copy-start | bytes 196612
  7.4 9.3 %copy-start.8 = (s32[1,2]{1,0:T(1,128)S(1)}, s32[1,2]{1,0:T(1,128)}, u32[]{:S(2)}) copy-start(s32[1,2]{1,0:T(1,128)} %param.22) | copy-start | bytes 28
  7.4 19.0 %copy-start.9 = (s32[1,128]{1,0:T(1,128)S(1)}, s32[1,128]{1,0:T(1,128)}, u32[]{:S(2)}) copy-start(s32[1,128]{1,0:T(1,128)} %param.21) | copy-start | bytes 1540
  7.4 19.8 %copy-start.11 = (s32[1,128,1]{1,2,0:T(1,128)S(1)}, s32[1,128,1]{1,2,0:T(1,128)}, u32[]{:S(2)}) copy-start(s32[1,128,1]{1,2,0:T(1,128)} %param.19) | copy-start | bytes 1540
  7.4 19.8 %copy-start.10 = (s32[1,128]{1,0:T(1,128)S(1)}, s32[1,128]{1,0:T(1,128)}, u32[]{:S(2)}) copy-start(s32[1,128]{1,0:T(1,128)} %param.20) | copy-start | bytes 1540
  7.4 17.9 %reduce-scatter.2.cloned.1.call-start = ((), (), s32[]{:S(2)}) async-start(), calls=%async_computation.4 | async-start | bytes 786432 | tf_op jit(solution)/shard_map/reduce_scatter | solution.py:202
  14.4 235.3 %copy-start.4 = (f32[64,64,2,2,1]{0,1,2,3,4:T(8,128)S(1)}, f32[64,64,2,2,1]{0,1,2,3,4:T(8,128)}, u32[]{:S(2)}) copy-start(f32[64,64,2,2,1]{0,1,2,3,4:T(8,128)} %constant.116) | copy-start | bytes 196612
  15.8 64.1 %all-gather.4.cloned.1.call-start = ((), (), s32[]{:S(2)}) async-start(), calls=%async_computation.3 | async-start | bytes 2228224 | tf_op jit(solution)/shard_map/all_gather | solution.py:181
  16.7 125.8 %all-gather.6.cloned.1.call-start = ((), (), s32[]{:S(2)}) async-start(), calls=%async_computation.5 | async-start | bytes 2228224 | tf_op jit(solution)/shard_map/all_gather | solution.py:209
  249.7 25.7 %copy-start.2 = (f32[64,128,16,2,2,2]{1,2,4,5,3,0:T(8,128)S(1)}, f32[64,128,16,2,2,2]{1,2,4,5,3,0:T(8,128)}, u32[]{:S(2)}) copy-start(f32[64,128,16,2,2,2]{1,2,4,5,3,0:T(8,128)} %constant.107.clone) | copy-start | bytes 12582916
  311.7 124.7 %all-to-all-start = ((f32[16,2,2,128,128]{4,2,1,3,0:T(2,128)}), f32[16,2,2,128,128]{4,2,1,3,0:T(2,128)}, u32[]{:S(2)}, u32[]{:S(2)}) async-start(f32[16,2,2,128,128]{4,2,1,3,0:T(2,128)} %copy.45), calls=%async_computation.1 | async-start | bytes 8388608 | tf_op jit(solution)/shard_map/all_to_all | solution.py:247
  436.4 102.0 %all-to-all-start.1 = ((f32[16,2,2,128,128]{4,2,1,3,0:T(2,128)}), f32[16,2,2,128,128]{4,2,1,3,0:T(2,128)}, u32[]{:S(2)}, u32[]{:S(2)}) async-start(f32[16,2,2,128,128]{4,2,1,3,0:T(2,128)} %copy.52), calls=%async_computation.2 | async-start | bytes 8388608 | tf_op jit(solution)/shard_map/all_to_all | solution.py:247
  441.8 2.9 copy-start.5
  441.8 7.3 %copy-start.3 = (f32[16,2,64,2,2,1]{2,0,1,3,4,5:T(8,128)S(1)}, f32[16,2,64,2,2,1]{2,0,1,3,4,5:T(8,128)}, u32[]{:S(2)}) copy-start(f32[16,2,64,2,2,1]{2,0,1,3,4,5:T(8,128)} %constant.117) | copy-start | bytes 98308
  449.2 8.4 %copy-start = (f32[64,128,64,2]{1,2,3,0:T(8,128)S(1)}, f32[64,128,64,2]{1,2,3,0:T(8,128)}, u32[]{:S(2)}) copy-start(f32[64,128,64,2]{1,2,3,0:T(8,128)} %constant.106.clone) | copy-start | bytes 12582916
  538.4 8.4 %copy-start.1 = (f32[64,128,64,2]{1,2,3,0:T(8,128)S(1)}, f32[64,128,64,2]{1,2,3,0:T(8,128)}, u32[]{:S(2)}) copy-start(f32[64,128,64,2]{1,2,3,0:T(8,128)} %constant.106.clone) | copy-start | bytes 12582916
Sparse Core Ops, SparseCore 0:
  16.0 9.2 reduce-scatter.1
Sparse Core Ops, SparseCore 1:
  19.1 60.8 all-gather.3
  83.0 59.4 all-gather.5

commit v2 on v1

--- a/solution.py
+++ b/solution.py
@@ -40,8 +40,13 @@
     return jnp.exp(gap * gap * (-0.5 / (kernel_width * kernel_width)))
 
 
-def grid_kernel(band, codes, first, spots, values, out, edge, picked):
-    blocks = spots.shape[0]
+def reach(tile, first, width):
+    low = jnp.where(tile * TILE >= HALF, tile * TILE - HALF, HALF - tile * TILE - (TILE - 1))
+    return low, (low < first + width) & (low + TILE > first)
+
+
+def grid_kernel(band, group, skip, codes, first, payload, out, edge, picked):
+    blocks = codes.shape[0]
     width = out.shape[2]
     base_w = first[0]
     step = 256
@@ -55,20 +60,17 @@
 
     lax.fori_loop(0, NG // step, clear, 0)
 
-    def reach(tile):
-        low = jnp.where(tile * TILE >= HALF, tile * TILE - HALF, HALF - tile * TILE - (TILE - 1))
-        return low, (low < base_w + width) & (low + TILE > base_w)
-
     def pick(at, count):
         tile = lax.rem(codes[at], NG // TILE)
-        _, mine = reach(tile)
+        _, mine = reach(tile, base_w, width)
         picked[count] = at
         return count + jnp.where(mine | (tile == 0), 1, 0)
 
     count = lax.fori_loop(0, blocks, pick, 0, unroll=8)
     tall = band + PAD
+    piece = min(width, TILE)
     p_ids = lax.broadcasted_iota(jnp.int32, (tall, VISIBILITY_ROWS), 0)
-    w_ids = lax.broadcasted_iota(jnp.int32, (width, VISIBILITY_ROWS), 0)
+    w_ids = lax.broadcasted_iota(jnp.int32, (piece, VISIBILITY_ROWS), 0)
     e_ids = lax.broadcasted_iota(jnp.int32, (TILE, VISIBILITY_ROWS), 0)
 
     def product(left, right):
@@ -81,33 +83,43 @@
         code = codes[block]
         owner = lax.div(code, NG // TILE)
         tile = lax.rem(code, NG // TILE)
-        low, mine = reach(tile)
+        low, _ = reach(tile, base_w, width)
         mirrored = tile * TILE < HALF
         sign = jnp.where(mirrored, -1, 1)
-        eight = pl.ds(pl.multiple_of(lax.div(block, 8) * 8, 8), 8)
-        here = lax.broadcasted_iota(jnp.int32, (8, 2 * TILE), 0) == lax.rem(block, 8)
-        spot = jnp.sum(jnp.where(here, spots[eight, :], 0.0), axis=0, keepdims=True)
-        value_row = jnp.sum(jnp.where(here, values[eight, :], 0.0), axis=0, keepdims=True)
-        u, v = spot[:, :TILE], spot[:, TILE:]
-        real, imag = value_row[:, :TILE], value_row[:, TILE:] * sign.astype(jnp.float32)
-        j_ids = sign * p_ids + jnp.where(mirrored, band, 0)
+        row = block + skip * lax.div(block, group)
+        eight = pl.ds(pl.multiple_of(lax.div(row, 8) * 8, 8), 8)
+        here = lax.broadcasted_iota(jnp.int32, (8, 4 * TILE), 0) == lax.rem(row, 8)
+        fields = jnp.sum(jnp.where(here, payload[eight, :], 0.0), axis=0, keepdims=True)
+        real = fields[:, :TILE]
+        imag = fields[:, TILE : 2 * TILE] * sign.astype(jnp.float32)
+        u = fields[:, 2 * TILE : 3 * TILE]
+        v = fields[:, 3 * TILE :]
+        centre = jnp.where(mirrored, band - v, v)
+        least = jnp.where(mirrored, 1, 0)
         left = jnp.where(
-            (j_ids >= 0) & (j_ids < band), spread(j_ids.astype(jnp.float32) - v), 0.0
+            (p_ids >= least) & (p_ids < band + least),
+            spread(p_ids.astype(jnp.float32) - centre),
+            0.0,
         ).astype(jnp.bfloat16)
         start = jnp.where(mirrored, NG - band * (owner + 1), band * owner)
         main_rows = pl.ds(pl.multiple_of(start, band), band)
         last_rows = pl.ds(pl.multiple_of(lax.rem(start + band, NG), band), PAD)
 
-        @pl.when(mine)
-        def _():
-            i_ids = sign * (w_ids + base_w - low) + jnp.where(mirrored, TILE - 1, 0)
-            across = jnp.where(
-                (i_ids >= 0) & (i_ids < TILE), spread(i_ids.astype(jnp.float32) - u), 0.0
-            )
-            for part, value in ((0, real), (1, imag)):
-                made = product(left, (value * across).astype(jnp.bfloat16))
-                out[part, main_rows, :] += made[:band]
-                out[part, last_rows, :] += made[band:]
+        for at_w in range(0, width, piece):
+            columns = slice(at_w, at_w + piece)
+
+            @pl.when(reach(tile, base_w + at_w, piece)[1])
+            def _():
+                i_ids = sign * (w_ids + (base_w + at_w) - low) + jnp.where(mirrored, TILE - 1, 0)
+                across = jnp.where(
+                    (i_ids >= 0) & (i_ids < TILE), spread(i_ids.astype(jnp.float32) - u), 0.0
+                )
+                right = jnp.concatenate([real * across, imag * across], axis=0)
+                made = product(left, right.astype(jnp.bfloat16))
+                for part in (0, 1):
+                    mine = made[:, part * piece : (part + 1) * piece]
+                    out[part, main_rows, columns] += mine[:band]
+                    out[part, last_rows, columns] += mine[band:]
 
         @pl.when(tile == 0)
         def _():
@@ -124,20 +136,20 @@
     lax.fori_loop(0, count, add, 0)
 
 
-def grid_blocks(codes, first, spots, values, band, width):
+def grid_blocks(codes, first, payload, band, width, group, skip):
     vmem = pl.BlockSpec(memory_space=pltpu.VMEM)
     smem = pl.BlockSpec(memory_space=pltpu.SMEM)
     return pl.pallas_call(
-        functools.partial(grid_kernel, band),
+        functools.partial(grid_kernel, band, group, skip),
         out_shape=(
             jax.ShapeDtypeStruct((2, NG, width), jnp.float32),
             jax.ShapeDtypeStruct((NG, TILE), jnp.float32),
         ),
-        in_specs=[smem, smem, vmem, vmem],
+        in_specs=[smem, smem, vmem],
         out_specs=(vmem, vmem),
-        scratch_shapes=[pltpu.SMEM((spots.shape[0] + 8,), jnp.int32)],
+        scratch_shapes=[pltpu.SMEM((codes.shape[0] + 8,), jnp.int32)],
         compiler_params=pltpu.CompilerParams(vmem_limit_bytes=56 * 1024 * 1024),
-    )(codes, first, spots, values)
+    )(codes, first, payload)
 
 
 def taper(indices):
@@ -178,14 +190,18 @@
     antenna_pairs = visibilities.shape[4]
     local_block_count = local_bin_count * antenna_pairs // VISIBILITY_ROWS
     blocked = (local_block_count, VISIBILITY_ROWS)
-    spots = lax.all_gather(
-        jnp.concatenate([u_offset[0].reshape(blocked), v_offset[0].reshape(blocked)], axis=1),
-        "uv",
-        tiled=True,
-    )
-    codes = lax.all_gather(
-        block_owner[0, :, 0] * (NG // TILE) + block_u_tile[0], "uv", tiled=True
-    )
+    band = NG // owners
+    width = HALF // owners
+    me = lax.axis_index("uv")
+    tiles = block_u_tile[0]
+    codes = block_owner[0, :, 0] * (NG // TILE) + tiles
+    room = min(local_block_count, -(-(16 + 2 * local_block_count // owners) // 8) * 8)
+    starts = jnp.arange(owners)[:, None] * width
+    wanted = reach(tiles[None, :], starts, width)[1] | (tiles[None, :] == 0)
+    ranks = jnp.cumsum(wanted.astype(jnp.int32), axis=1) - 1
+    fullest = lax.pmax(jnp.max(ranks) + 1, ("tm", "uv"))
+    chosen = wanted[:, None, :] & (ranks[:, None, :] == jnp.arange(room)[None, :, None])
+    sent_codes = jnp.sum(jnp.where(chosen, codes + 1, 0), axis=2)
     real_part = visibilities[:, :, :, 0].astype(jnp.float32)
     imag_part = visibilities[:, :, :, 1].astype(jnp.float32)
     powers = real_part * real_part + imag_part * imag_part
@@ -206,15 +222,30 @@
     live_rows = jnp.arange(VISIBILITY_ROWS)[None, :] < block_count[0][:, None]
     avg_real = jnp.where(live_rows, avg_real, 0.0)
     avg_imag = jnp.where(live_rows, avg_imag, 0.0)
-    values = lax.all_gather(
-        jnp.concatenate([avg_real, avg_imag], axis=1), "uv", tiled=True
-    )
-    band = NG // owners
-    width = HALF // owners
-    me = lax.axis_index("uv")
-    uv_grid, edge = grid_blocks(
-        codes, (me * width)[None].astype(jnp.int32), spots, values, band, width
-    )
+    payload = jnp.concatenate(
+        [avg_real, avg_imag, u_offset[0].reshape(blocked), v_offset[0].reshape(blocked)], axis=1
+    )
+    first = (me * width)[None].astype(jnp.int32)
+
+    def to_reached(payload):
+        sent = jnp.einsum(
+            "esb,bf->esf", chosen.astype(jnp.float32), payload, precision=lax.Precision.HIGHEST
+        )
+        line = jnp.pad(sent_codes.astype(jnp.float32), ((0, 0), (0, payload.shape[1] - room)))
+        lines = jnp.pad(line[:, None, :], ((0, 0), (0, 7), (0, 0)))
+        got = lax.all_to_all(
+            jnp.concatenate([sent, lines], axis=1), "uv", split_axis=0, concat_axis=0, tiled=True
+        )
+        got_codes = got[:, room, :room].astype(jnp.int32).reshape(-1) - 1
+        rows = got.reshape(owners * (room + 8), payload.shape[1])
+        return grid_blocks(got_codes, first, rows, band, width, room, 8)
+
+    def to_all(payload):
+        every = lax.all_gather(payload, "uv", tiled=True)
+        every_code = lax.all_gather(codes, "uv", tiled=True)
+        return grid_blocks(every_code, first, every, band, width, local_block_count, 0)
+
+    uv_grid, edge = lax.cond(fullest <= room, to_reached, to_all, payload)
 
     outer = NG // TILE
     one, two = transform_tables(TILE, outer)
@@ -236,19 +267,22 @@
     row_two = row_two[..., 0]
     scale = 1.0 / math.sqrt(NBIN * BL_DEV * owners)
     col_ids = jnp.arange(NI)
-    parts = 2 if jj_mine % 2 == 0 else 1
-    jj_part = jj_mine // parts
-    rows_part = rows_mine // parts
+    quarter = jj_mine // 4
+    parts = (quarter, 2 * quarter, quarter) if jj_mine % 4 == 0 else (jj_mine,)
     images = []
-    for part in range(parts):
-        table = two_split[:, :, :, part * jj_part : (part + 1) * jj_part]
+    jj_done = 0
+    for jj_part in parts:
+        rows_part = jj_part * outer
+        rows_done = jj_done * outer
+        table = two_split[:, :, :, jj_done : jj_done + jj_part]
+        jj_done += jj_part
         columns = mix("ckqw,kqejcd->edjkw", stage, table)
         columns = columns.reshape(owners, 2, rows_part, per_owner, inner).transpose(0, 1, 3, 2, 4)
         columns = lax.all_to_all(columns, "uv", split_axis=0, concat_axis=0, tiled=True)
         row_stage = mix("scnmq,snkcd->dkmq", columns, row_one)
         image = mix("ckmq,kqjc->mjk", row_stage, row_two).reshape(rows_part, NI)
-        row_ids = me * rows_mine + part * rows_part + jnp.arange(rows_part)
-        edge_part = edge_mine[part * rows_part : (part + 1) * rows_part]
+        row_ids = me * rows_mine + rows_done + jnp.arange(rows_part)
+        edge_part = edge_mine[rows_done : rows_done + rows_part]
         col_sign = 1.0 - 2.0 * (col_ids % 2).astype(jnp.float32)
         row_sign = 1.0 - 2.0 * (row_ids % 2).astype(jnp.float32)
         image = image + edge_part[:, None] * col_sign[None, :]

time: 578 us -> 515 us (0.89)
  waiting for transfers between devices: 220 us -> 86.6 us
  blocking collectives: 29.1 us -> 75.5 us
  matrix products: 106 us -> 127 us
  Pallas kernels: 107 us -> 89.4 us
  local copies, waits for them, and re-layouts: 44.8 us -> 56.3 us
  starting transfers between devices: 36.5 us -> 43.4 us
    all_gather x2 -> x0, waiting for transfers between devices: 86.2 us -> none  [the longest x1 62.5 us: body(): lax.all_gather(jnp.concatenate([avg_real, avg_imag], axis=1), 'uv', tiled...]
    pmax x0 -> x1, blocking collectives: none -> 40.6 us  [body(): fullest = lax.pmax(jnp.max(ranks) + 1, ('tm', 'uv'))]
    all_to_all x2 -> x3, waiting for transfers between devices: 127 us -> 86.6 us  [body(): lax.all_to_all(columns, 'uv', split_axis=0, concat_axis=0, tiled=True)]
    all_to_all x0 -> x1, blocking collectives: none -> 34.9 us  [to_reached(): lax.all_to_all(jnp.concatenate([sent, lines], axis=1), 'uv', split_axis=0...]
    all_gather x1 -> x0, blocking collectives: 29.1 us -> none  [body(): lax.all_gather(block_owner[0, :, 0] * (NG // TILE) + block_u_tile[0], 'uv...]
    dot_general x2 -> x3, matrix products: 42 us -> 62.9 us  [body(): columns = mix('ckqw,kqejcd->edjkw', stage, table)]
    pallas_call x1, Pallas kernels: 107 us -> 89.4 us  [grid_blocks(): pl.pallas_call(functools.partial(grid_kernel, band, group, skip), out_sha...]
    reshape x2 -> x5, local copies, waits for them, and re-layouts: 11.7 us -> 19.6 us  [body(): columns.reshape(owners, 2, rows_part, per_owner, inner)]
  transfers between devices with their start and end apart: 5 -> 4, of which waited for: 5 -> 3; matrix products, arithmetic and copies ran while one was open for 12% -> 21% of each run, Pallas kernels for 0% -> 0%
where the time goes in v2:
time: 515 us; the launch traced here: 513 us
  matrix products  127 us (25%)
  Pallas kernels  89.4 us (17%)
  waiting for transfers between devices  86.6 us (17%)
  blocking collectives  75.5 us (15%)
  local copies, waits for them, and re-layouts  56.3 us (11%)
  starting transfers between devices  43.4 us (8%)
  other arithmetic  17.9 us (3%)
  between operations  16.5 us (3%)
    pallas_call x1, Pallas kernels, grid_blocks(): pl.pallas_call(functools.partial(grid_kernel, band, group, skip), out_sha...  89.4 us
    all_to_all x3, waiting for transfers between devices, body(): lax.all_to_all(columns, 'uv', split_axis=0, concat_axis=0, tiled=True)  86.6 us
    dot_general x3, matrix products, body(): columns = mix('ckqw,kqejcd->edjkw', stage, table)  62.9 us
    all_to_all x3, starting transfers between devices, body(): lax.all_to_all(columns, 'uv', split_axis=0, concat_axis=0, tiled=True)  43.3 us
    pmax x1, blocking collectives, body(): fullest = lax.pmax(jnp.max(ranks) + 1, ('tm', 'uv'))  40.6 us
    all_to_all x1, blocking collectives, to_reached(): lax.all_to_all(jnp.concatenate([sent, lines], axis=1), 'uv', split_axis=0...  34.9 us
    dot_general x1, matrix products, body(): stage = mix('cnqw,nkcd->dkqw', uv_grid.reshape(2, outer, TILE, width), one)  25.8 us
    reshape x5, local copies, waits for them, and re-layouts, body(): columns.reshape(owners, 2, rows_part, per_owner, inner)  19.6 us
  transfers between devices with their start and end apart: 4, of which 3 were waited for; matrix products, arithmetic and copies ran while one was open for 21% of the time, Pallas kernels for 0%

profile of v2, /device:TPU:14, one launch (start us, length us, event | category | flops | bytes accessed | tf_op | source)
XLA Modules:
  0.0 512.9 jit_solution(15583015318378145513)
XLA Ops:
  6.6 5.1 convert_reduce_fusion.1
  11.7 1.9 fusion.81
  13.9 1.1 copy.55
  15.4 0.7 broadcast_add_fusion.1
  16.7 40.6 %pmax.7 = s32[]{:T(128)} all-reduce(s32[]{:T(128)S(6)} %add.165), channel_id=1, replica_groups=mesh['tm'=2,'uv'=16] {'tm','uv'}, use_global_device_ids=true, to_apply=%region_2.3 | all-reduce | flops 1 | bytes 8 | tf_op jit(solution)/shard_map/pmax | solution.py:202
  57.3 0.6 fusion.83
  59.8 1.0 fusion.46
  61.0 126.7 %conditional.1 = (f32[8192,128]{1,0:T(8,128)}, f32[2,64,128,256]{3,2,1,0:T(8,128)}) conditional(s32[]{:T(128)} %convert_element_type.104, (s32[128]{0:T(128)S(1)}, f32[128,512]{1,0:T(8,128)S(1)}, s32[1]{0:T(128)}) %tuple.15, (pred[16,128]{1,0:T(8,128)(4,1)S(1)}, s32[16,128]{1,0:T(8,128)S(1)}, s32[16,32,128]{2,1,0:T(8,128)S(1)}, ...), branch_computations={%region_8.9_spmd, %region_9.11_spmd} | conditional | flops 403899520 | bytes 14426708 | solution.py:248
  61.5 0.6 fusion
  62.2 34.9 %all_to_all.19 = f32[16,40,512]{2,1,0:T(8,128)S(1)} all-to-all(f32[16,40,512]{2,1,0:T(8,128)S(1)} %select_maximum_fusion), channel_id=1, replica_groups=mesh['tm'=2,'uv'=16] {'uv'}, dimensions={0} | all-to-all | bytes 2621440 | tf_op jit(solution)/shard_map/cond/branch_1_fun/all_to_all | solution.py:236
  97.2 0.8 sub.72.codes
  98.2 89.4 %branch_1_fun.1 = (f32[2,8192,256]{2,1,0:T(8,128)}, f32[8192,128]{1,0:T(8,128)}) custom-call(s32[512]{0:T(512)} %sub.72.codes, s32[1]{0:T(128)} %get-tuple-element.52.first, f32[640,512]{1,0:T(8,128)} %bitcast.166), custom_call_target="tpu_custom_call" | custom-call | tf_op jit(solution)/shard_map/cond/branch_1_fun/pallas_call | solution.py:142
  187.8 25.8 %fusion.6 = f32[128,256,64,2,1]{1,2,4,3,0:T(8,128)} fusion(f32[64,64,2,2,1]{0,1,2,3,4:T(8,128)S(1)} %copy-done.8, f32[2,64,128,256,1]{3,2,1,0,4:T(8,128)} %bitcast.161), kind=kOutput, calls=%fused_computation.12 | convolution fusion | flops 3221225472 | bytes 33619968 | tf_op jit(solution)/shard_map/cnqw,nkcd->dkqw/dot_general | solution.py:254
  213.5 19.6 %fusion.33 = f32[16,2,1,64,256]{4,0,1,3,2:T(8,128)S(1)} fusion(f32[64,128,16,2,2]{1,2,3,4,0:T(8,128)S(1)} %copy-done.6, f32[2,64,128,256,1]{3,1,0,2,4:T(8,128)} %bitcast.156), kind=kOutput, calls=%fused_computation.39 | convolution fusion | flops 805306368 | bytes 20971520 | tf_op jit(solution)/shard_map/ckqw,kqejcd->edjkw/dot_general | solution.py:279
  233.1 2.1 reshape.270
  235.3 4.0 copy.151
  239.3 32.8 %all-to-all-start.1 = ((f32[16,2,2,64,128]{4,2,1,3,0:T(2,128)}), f32[16,2,2,64,128]{4,2,1,3,0:T(2,128)S(1)}, u32[]{:S(2)}, u32[]{:S(2)}) async-start(f32[16,2,2,64,128]{4,2,1,3,0:T(2,128)} %bitcast.165), calls=%async_computation.2 | async-start | bytes 4194304 | tf_op jit(solution)/shard_map/all_to_all | solution.py:281
  272.1 21.6 %fusion.36 = f32[16,2,1,64,256]{4,0,1,3,2:T(8,128)} fusion(f32[64,128,16,2,2]{1,2,3,4,0:T(8,128)} %constant.176, f32[2,64,128,256,1]{3,1,0,2,4:T(8,128)} %bitcast.157), kind=kOutput, calls=%fused_computation.40 | convolution fusion | flops 805306368 | bytes 20971520 | tf_op jit(solution)/shard_map/ckqw,kqejcd->edjkw/dot_general | solution.py:279
  293.7 3.3 reshape.276
  296.9 4.0 copy.150
  300.9 19.4 %all-to-all-done.1 = f32[16,2,2,64,128]{4,2,1,3,0:T(2,128)S(1)} async-done(((f32[16,2,2,64,128]{4,2,1,3,0:T(2,128)}), f32[16,2,2,64,128]{4,2,1,3,0:T(2,128)S(1)}, u32[]{:S(2)}, u32[]{:S(2)}) %all-to-all-start.1) | async-done | bytes 2097184 | tf_op jit(solution)/shard_map/all_to_all | solution.py:281
  320.4 5.4 %all-to-all-start.3 = ((f32[16,2,2,64,128]{4,2,1,3,0:T(2,128)}), f32[16,2,2,64,128]{4,2,1,3,0:T(2,128)}, u32[]{:S(2)}, u32[]{:S(2)}) async-start(f32[16,2,2,64,128]{4,2,1,3,0:T(2,128)} %bitcast.164), calls=%async_computation.4 | async-start | bytes 4194304 | tf_op jit(solution)/shard_map/all_to_all | solution.py:281
  325.8 21.7 %fusion.23 = f32[16,2,2,64,256]{4,0,1,2,3:T(8,128)S(1)} fusion(f32[64,128,16,2,2,2]{1,2,4,5,3,0:T(8,128)} %constant.163.clone, f32[2,64,128,256,1,1]{3,1,0,2,5,4:T(8,128)} %bitcast.158), kind=kOutput, calls=%fused_computation.28 | convolution fusion | flops 1610612736 | bytes 25165824 | tf_op jit(solution)/shard_map/ckqw,kqejcd->edjkw/dot_general | solution.py:279
  347.5 4.4 copy.64
  351.9 6.2 %reshape.273 = f32[16,2,128,2,128]{4,3,2,1,0:T(2,128)} reshape(f32[16,2,2,64,256]{4,3,2,1,0:T(8,128)} %copy.64) | data formatting | bytes 8388608 | tf_op jit(solution)/shard_map/reshape | solution.py:280
  358.1 5.6 %copy.65 = f32[16,2,2,128,128]{4,2,1,3,0:T(2,128)} copy(f32[16,2,2,128,128]{4,2,3,1,0:T(2,128)} %bitcast.162) | data formatting | bytes 8388608 | tf_op jit(solution)/shard_map/transpose | solution.py:280
  363.7 12.2 %all-to-all-done.3 = f32[16,2,2,64,128]{4,2,1,3,0:T(2,128)} async-done(((f32[16,2,2,64,128]{4,2,1,3,0:T(2,128)}), f32[16,2,2,64,128]{4,2,1,3,0:T(2,128)}, u32[]{:S(2)}, u32[]{:S(2)}) %all-to-all-start.3) | async-done | bytes 2097184 | tf_op jit(solution)/shard_map/all_to_all | solution.py:281
  376.0 5.1 all-to-all-start.2
  381.2 2.9 copy.103
  384.3 3.9 fusion.53
  388.5 2.9 convolution_bitcast_fusion.1
  391.4 4.5 fusion.39
  396.0 2.2 copy.61
  398.2 2.3 reshape.271
  400.5 4.6 convolution_bitcast_fusion
  405.1 4.5 fusion.42
  409.7 2.2 copy.73
  411.9 2.1 reshape.277
  414.1 1.8 multiply_divide_fusion.1
  415.9 1.8 copy.74
  417.7 3.2 copy.75
  420.9 54.9 %all-to-all-done.2 = f32[16,2,2,128,128]{4,2,1,3,0:T(2,128)} async-done(((f32[16,2,2,128,128]{4,2,1,3,0:T(2,128)}), f32[16,2,2,128,128]{4,2,1,3,0:T(2,128)}, u32[]{:S(2)}, u32[]{:S(2)}) %all-to-all-start.2) | async-done | bytes 4194336 | tf_op jit(solution)/shard_map/all_to_all | solution.py:281
  475.8 8.4 %fusion.20 = f32[2,64,128,128]{3,1,0,2:T(8,128)S(1)} fusion(f32[16,2,64,2,2,1]{2,0,1,3,4,5:T(8,128)S(1)} %copy-done.7, f32[16,2,2,128,128,1]{4,2,1,3,0,5:T(2,128)} %bitcast.55), kind=kOutput, calls=%fused_computation.27 | convolution fusion | flops 805306368 | bytes 12615680 | tf_op jit(solution)/shard_map/scnmq,snkcd->dkmq/dot_general | solution.py:282
  484.1 8.8 %fusion.30 = f32[128,64,64]{0,1,2:T(8,128)S(1)} fusion(f32[64,128,64,2]{1,2,3,0:T(8,128)S(1)} %copy-done.2, f32[2,64,128,128]{3,1,0,2:T(8,128)S(1)} %fusion.20), kind=kOutput, calls=%fused_computation.38 | convolution fusion | flops 805306368 | bytes 14680064 | tf_op jit(solution)/shard_map/ckmq,kqjc->mjk/dot_general | solution.py:283
  492.9 1.2 copy.68
  494.1 2.4 fusion.28
  496.6 3.7 maximum_bitcast_fusion
  500.2 5.6 %copy.76 = f32[1,256,4096]{2,1,0:T(8,128)} copy(f32[1,256,4096]{1,2,0:T(8,128)} %maximum_bitcast_fusion) | data formatting | bytes 8388608 | tf_op jit(solution)/shard_map/broadcast_in_dim | solution.py:291
  (63 shorter events, 2.3 us)
Async XLA Ops:
  6.5 8.5 %copy-start.14 = (s32[1,128]{1,0:T(1,128)S(1)}, s32[1,128]{1,0:T(1,128)}, u32[]{:S(2)}) copy-start(s32[1,128]{1,0:T(1,128)} %param.25) | copy-start | bytes 1540
  6.5 50.8 %copy-start.12 = (s32[1,2]{1,0:T(1,128)S(1)}, s32[1,2]{1,0:T(1,128)}, u32[]{:S(2)}) copy-start(s32[1,2]{1,0:T(1,128)} %param.27) | copy-start | bytes 28
  6.5 52.5 %copy-start.10 = (f32[1,8,2048]{2,1,0:T(8,128)S(1)}, f32[1,8,2048]{2,1,0:T(8,128)}, u32[]{:S(2)}) copy-start(f32[1,8,2048]{2,1,0:T(8,128)} %param.22) | copy-start | bytes 196612
  6.5 52.6 %copy-start.11 = (f32[1,8,2048]{2,1,0:T(8,128)S(1)}, f32[1,8,2048]{2,1,0:T(8,128)}, u32[]{:S(2)}) copy-start(f32[1,8,2048]{2,1,0:T(8,128)} %param.23) | copy-start | bytes 196612
  6.5 53.2 %copy-start.15 = (s32[1,128,1]{1,2,0:T(1,128)S(1)}, s32[1,128,1]{1,2,0:T(1,128)}, u32[]{:S(2)}) copy-start(s32[1,128,1]{1,2,0:T(1,128)} %param.24) | copy-start | bytes 1540
  6.5 54.3 %copy-start.13 = (s32[1,128]{1,0:T(1,128)S(1)}, s32[1,128]{1,0:T(1,128)}, u32[]{:S(2)}) copy-start(s32[1,128]{1,0:T(1,128)} %param.26) | copy-start | bytes 1540
  6.6 53.3 %reduce-scatter.2.cloned.1.call-start = ((), (), s32[]{:S(2)}) async-start(), calls=%async_computation.6 | async-start | bytes 786432 | tf_op jit(solution)/shard_map/reduce_scatter | solution.py:218
  61.0 126.8 %copy-start.8 = (f32[64,64,2,2,1]{0,1,2,3,4:T(8,128)S(1)}, f32[64,64,2,2,1]{0,1,2,3,4:T(8,128)}, u32[]{:S(2)}) copy-start(f32[64,64,2,2,1]{0,1,2,3,4:T(8,128)} %constant.177) | copy-start | bytes 196612
  97.1 1.1 copy-start.4
  187.8 25.8 %copy-start.6 = (f32[64,128,16,2,2]{1,2,3,4,0:T(8,128)S(1)}, f32[64,128,16,2,2]{1,2,3,4,0:T(8,128)}, u32[]{:S(2)}) copy-start(f32[64,128,16,2,2]{1,2,3,4,0:T(8,128)} %constant.175) | copy-start | bytes 6291460
  239.3 81.1 %all-to-all-start.1 = ((f32[16,2,2,64,128]{4,2,1,3,0:T(2,128)}), f32[16,2,2,64,128]{4,2,1,3,0:T(2,128)S(1)}, u32[]{:S(2)}, u32[]{:S(2)}) async-start(f32[16,2,2,64,128]{4,2,1,3,0:T(2,128)} %bitcast.165), calls=%async_computation.2 | async-start | bytes 4194304 | tf_op jit(solution)/shard_map/all_to_all | solution.py:281
  320.4 55.6 %all-to-all-start.3 = ((f32[16,2,2,64,128]{4,2,1,3,0:T(2,128)}), f32[16,2,2,64,128]{4,2,1,3,0:T(2,128)}, u32[]{:S(2)}, u32[]{:S(2)}) async-start(f32[16,2,2,64,128]{4,2,1,3,0:T(2,128)} %bitcast.164), calls=%async_computation.4 | async-start | bytes 4194304 | tf_op jit(solution)/shard_map/all_to_all | solution.py:281
  376.0 99.8 %all-to-all-start.2 = ((f32[16,2,2,128,128]{4,2,1,3,0:T(2,128)}), f32[16,2,2,128,128]{4,2,1,3,0:T(2,128)}, u32[]{:S(2)}, u32[]{:S(2)}) async-start(f32[16,2,2,128,128]{4,2,1,3,0:T(2,128)} %copy.65), calls=%async_computation.3 | async-start | bytes 8388608 | tf_op jit(solution)/shard_map/all_to_all | solution.py:281
  381.1 3.0 copy-start.9
  381.2 7.3 %copy-start.7 = (f32[16,2,64,2,2,1]{2,0,1,3,4,5:T(8,128)S(1)}, f32[16,2,64,2,2,1]{2,0,1,3,4,5:T(8,128)}, u32[]{:S(2)}) copy-start(f32[16,2,64,2,2,1]{2,0,1,3,4,5:T(8,128)} %constant.178) | copy-start | bytes 98308
  388.5 2.9 copy-start
  400.5 4.6 copy-start.1
  475.8 8.4 %copy-start.2 = (f32[64,128,64,2]{1,2,3,0:T(8,128)S(1)}, f32[64,128,64,2]{1,2,3,0:T(8,128)}, u32[]{:S(2)}) copy-start(f32[64,128,64,2]{1,2,3,0:T(8,128)} %constant.160.clone) | copy-start | bytes 12582916
  492.9 3.7 copy-start.3
Sparse Core Ops, SparseCore 0:
  15.1 9.2 reduce-scatter.1

commit v3 on v2

--- a/solution.py
+++ b/solution.py
@@ -199,7 +199,7 @@
     starts = jnp.arange(owners)[:, None] * width
     wanted = reach(tiles[None, :], starts, width)[1] | (tiles[None, :] == 0)
     ranks = jnp.cumsum(wanted.astype(jnp.int32), axis=1) - 1
-    fullest = lax.pmax(jnp.max(ranks) + 1, ("tm", "uv"))
+    too_many = (jnp.max(ranks) + 1 > room).astype(jnp.float32)
     chosen = wanted[:, None, :] & (ranks[:, None, :] == jnp.arange(room)[None, :, None])
     sent_codes = jnp.sum(jnp.where(chosen, codes + 1, 0), axis=2)
     real_part = visibilities[:, :, :, 0].astype(jnp.float32)
@@ -215,6 +215,8 @@
         axis=0,
     )
     local_sums = local_sums.transpose(2, 0, 1, 3)
+    flag_plane = jnp.broadcast_to(too_many, local_sums[:, :1].shape)
+    local_sums = jnp.concatenate([local_sums, flag_plane], axis=1)
     totals = lax.psum_scatter(local_sums, "tm", scatter_dimension=0, tiled=True)[0]
     weight = kurtosis_weight(totals[2], totals[3], sk_window[0])
     avg_real = (weight * totals[0] / SUBS).reshape(blocked)
@@ -227,25 +229,33 @@
     )
     first = (me * width)[None].astype(jnp.int32)
 
-    def to_reached(payload):
-        sent = jnp.einsum(
-            "esb,bf->esf", chosen.astype(jnp.float32), payload, precision=lax.Precision.HIGHEST
-        )
-        line = jnp.pad(sent_codes.astype(jnp.float32), ((0, 0), (0, payload.shape[1] - room)))
-        lines = jnp.pad(line[:, None, :], ((0, 0), (0, 7), (0, 0)))
-        got = lax.all_to_all(
-            jnp.concatenate([sent, lines], axis=1), "uv", split_axis=0, concat_axis=0, tiled=True
-        )
+    sent = jnp.einsum(
+        "esb,bf->esf", chosen.astype(jnp.float32), payload, precision=lax.Precision.HIGHEST
+    )
+    line = jnp.concatenate(
+        [
+            sent_codes.astype(jnp.float32),
+            jnp.broadcast_to(totals[4, 0, 0], (owners, payload.shape[1] - room)),
+        ],
+        axis=1,
+    )
+    lines = jnp.pad(line[:, None, :], ((0, 0), (0, 7), (0, 0)))
+    got = lax.all_to_all(
+        jnp.concatenate([sent, lines], axis=1), "uv", split_axis=0, concat_axis=0, tiled=True
+    )
+    overfull = jnp.max(got[:, room, room])
+
+    def from_reaching(got, payload):
         got_codes = got[:, room, :room].astype(jnp.int32).reshape(-1) - 1
         rows = got.reshape(owners * (room + 8), payload.shape[1])
         return grid_blocks(got_codes, first, rows, band, width, room, 8)
 
-    def to_all(payload):
+    def from_all(got, payload):
         every = lax.all_gather(payload, "uv", tiled=True)
         every_code = lax.all_gather(codes, "uv", tiled=True)
         return grid_blocks(every_code, first, every, band, width, local_block_count, 0)
 
-    uv_grid, edge = lax.cond(fullest <= room, to_reached, to_all, payload)
+    uv_grid, edge = lax.cond(overfull < 0.5, from_reaching, from_all, got, payload)
 
     outer = NG // TILE
     one, two = transform_tables(TILE, outer)

time: 515 us -> 481 us (0.934)
  blocking collectives: 75.5 us -> 0 us
  waiting for transfers between devices: 86.6 us -> 123 us
  Pallas kernels: 89.4 us -> 102 us
  starting transfers between devices: 43.4 us -> 33.8 us
    pmax x1 -> x0, blocking collectives: 40.6 us -> none  [body(): fullest = lax.pmax(jnp.max(ranks) + 1, ('tm', 'uv'))]
    all_to_all x1 -> x0, blocking collectives: 34.9 us -> none  [to_reached(): lax.all_to_all(jnp.concatenate([sent, lines], axis=1), 'uv', split_axis=0...]
    all_to_all x0 -> x1, waiting for transfers between devices: none -> 31.2 us  [body(): lax.all_to_all(jnp.concatenate([sent, lines], axis=1), 'uv', split_axis=0...]
    all_to_all x3, starting transfers between devices: 43.3 us -> 26.7 us  [body(): lax.all_to_all(columns, 'uv', split_axis=0, concat_axis=0, tiled=True)]
    pallas_call x1, Pallas kernels: 89.4 us -> 102 us  [grid_blocks(): pl.pallas_call(functools.partial(grid_kernel, band, group, skip), out_sha...]
    reduce_scatter x1, waiting for transfers between devices: 0.02 us -> 7.33 us  [body(): lax.psum_scatter(local_sums, 'tm', scatter_dimension=0, tiled=True)[0]]
    all_to_all x0 -> x1, starting transfers between devices: none -> 7.08 us  [body(): lax.all_to_all(jnp.concatenate([sent, lines], axis=1), 'uv', split_axis=0...]
  transfers between devices with their start and end apart: 4 -> 5, of which waited for: 3 -> 5; matrix products, arithmetic and copies ran while one was open for 21% -> 22% of each run, Pallas kernels for 0% -> 0%
where the time goes in v3:
time: 481 us
  matrix products  127 us (26%)
  waiting for transfers between devices  123 us (26%)
  Pallas kernels  102 us (21%)
  local copies, waits for them, and re-layouts  57.8 us (12%)
  starting transfers between devices  33.8 us (7%)
  other arithmetic  20.9 us (4%)
  between operations  16.6 us (3%)
    pallas_call x1, Pallas kernels, grid_blocks(): pl.pallas_call(functools.partial(grid_kernel, band, group, skip), out_sha...  102 us
    all_to_all x3, waiting for transfers between devices, body(): lax.all_to_all(columns, 'uv', split_axis=0, concat_axis=0, tiled=True)  84.6 us
    dot_general x3, matrix products, body(): columns = mix('ckqw,kqejcd->edjkw', stage, table)  62.9 us
    all_to_all x1, waiting for transfers between devices, body(): lax.all_to_all(jnp.concatenate([sent, lines], axis=1), 'uv', split_axis=0...  31.2 us
    all_to_all x3, starting transfers between devices, body(): lax.all_to_all(columns, 'uv', split_axis=0, concat_axis=0, tiled=True)  26.7 us
    dot_general x1, matrix products, body(): stage = mix('cnqw,nkcd->dkqw', uv_grid.reshape(2, outer, TILE, width), one)  25.7 us
    reshape x5, local copies, waits for them, and re-layouts, body(): columns.reshape(owners, 2, rows_part, per_owner, inner)  19.6 us
    dot_general x3, matrix products, body(): image = mix('ckmq,kqjc->mjk', row_stage, row_two).reshape(rows_part, NI)  17.9 us
  transfers between devices with their start and end apart: 5, of which 5 were waited for; matrix products, arithmetic and copies ran while one was open for 22% of the time, Pallas kernels for 0%

profile of v3, /device:TPU:14, one launch (start us, length us, event | category | flops | bytes accessed | tf_op | source)
XLA Modules:
  0.0 481.4 jit_solution(15068586975957437499)
XLA Ops:
  7.9 5.1 %convert_reduce_fusion.1 = (f32[8,2,2048]{2,1,0:T(2,128)S(1)}, f32[8,2,2048]{2,1,0:T(2,128)S(1)}, f32[8,8,2,1,2048]{4,3,2,1,0:T(1,128)S(1)}) fusion(bf16[8,8,2,2,2048]{4,3,2,1,0:T(2,128)(2,1)} %param.21), kind=kLoop, calls=%fused_computation.42 | loop fusion | flops 1769472 | bytes 2359296 | tf_op jit(solution)/shard_map/reduce_sum | solution.py:210
  13.0 1.9 fusion.83
  17.1 0.9 concatenate.15.clone
  20.3 7.3 %reduce-scatter.2.cloned.1.call-done = f32[1,5,8,2048]{3,2,1,0:T(8,128)} async-done(((f32[2,5,8,2048]{3,2,1,0:T(8,128)}), f32[1,5,8,2048]{3,2,1,0:T(8,128)}) %reduce-scatter.2.cloned.1.call-update) | async-done | bytes 327696 | tf_op jit(solution)/shard_map/reduce_scatter | solution.py:220
  27.6 1.0 fusion.48
  28.7 1.2 slice.72
  31.2 1.2 select_maximum_fusion
  32.5 7.1 %all-to-all-start = ((f32[16,40,512]{2,1,0:T(8,128)}), f32[16,40,512]{2,1,0:T(8,128)S(1)}, u32[]{:S(2)}, u32[]{:S(2)}) async-start(f32[16,40,512]{2,1,0:T(8,128)} %select_maximum_fusion), calls=%async_computation.1 | async-start | bytes 2621440 | tf_op jit(solution)/shard_map/all_to_all | solution.py:243
  39.6 31.2 %all-to-all-done = f32[16,40,512]{2,1,0:T(8,128)S(1)} async-done(((f32[16,40,512]{2,1,0:T(8,128)}), f32[16,40,512]{2,1,0:T(8,128)S(1)}, u32[]{:S(2)}, u32[]{:S(2)}) %all-to-all-start) | async-done | bytes 1310752 | tf_op jit(solution)/shard_map/all_to_all | solution.py:243
  70.8 0.7 slice_reduce_fusion
  72.1 102.7 %conditional.1 = (f32[8192,128]{1,0:T(8,128)}, f32[2,64,128,256]{3,2,1,0:T(8,128)}) conditional(s32[]{:T(128)} %convert_element_type.111, (s32[128]{0:T(128)S(1)}, f32[128,512]{1,0:T(8,128)S(1)}, s32[1]{0:T(128)}) %tuple.15, (f32[16,40,512]{2,1,0:T(8,128)S(1)}, s32[1]{0:T(128)}) %tuple.16), branch_computations={%region_9.10_spmd, %region_10.11_spmd} | conditional | flops 1024 | bytes 14426708 | solution.py:258
  72.9 101.8 %branch_1_fun.1 = (f32[2,8192,256]{2,1,0:T(8,128)}, f32[8192,128]{1,0:T(8,128)}) custom-call(s32[512]{0:T(512)} %sub.72.codes, s32[1]{0:T(128)} %get-tuple-element.26.first, f32[640,512]{1,0:T(8,128)S(1)} %bitcast.169), custom_call_target="tpu_custom_call" | custom-call | tf_op jit(solution)/shard_map/cond/branch_1_fun/pallas_call | solution.py:142
  174.9 25.7 %fusion.2 = f32[128,256,64,2,1]{1,2,4,3,0:T(8,128)} fusion(f32[64,64,2,2,1]{0,1,2,3,4:T(8,128)S(1)} %copy-done.7, f32[2,64,128,256,1]{3,2,1,0,4:T(8,128)} %bitcast.164), kind=kOutput, calls=%fused_computation.3 | convolution fusion | flops 3221225472 | bytes 33619968 | tf_op jit(solution)/shard_map/cnqw,nkcd->dkqw/dot_general | solution.py:264
  200.6 19.6 %fusion.29 = f32[16,2,1,64,256]{4,0,1,3,2:T(8,128)S(1)} fusion(f32[64,128,16,2,2]{1,2,3,4,0:T(8,128)S(1)} %copy-done.4, f32[2,64,128,256,1]{3,1,0,2,4:T(8,128)} %bitcast.159), kind=kOutput, calls=%fused_computation.30 | convolution fusion | flops 805306368 | bytes 20971520 | tf_op jit(solution)/shard_map/ckqw,kqejcd->edjkw/dot_general | solution.py:289
  220.2 2.1 reshape.270
  222.3 4.0 copy.152
  226.3 16.1 %all-to-all-start.1 = ((f32[16,2,2,64,128]{4,2,1,3,0:T(2,128)}), f32[16,2,2,64,128]{4,2,1,3,0:T(2,128)S(1)}, u32[]{:S(2)}, u32[]{:S(2)}) async-start(f32[16,2,2,64,128]{4,2,1,3,0:T(2,128)} %bitcast.168), calls=%async_computation.2 | async-start | bytes 4194304 | tf_op jit(solution)/shard_map/all_to_all | solution.py:291
  242.5 21.6 %fusion.32 = f32[16,2,1,64,256]{4,0,1,3,2:T(8,128)} fusion(f32[64,128,16,2,2]{1,2,3,4,0:T(8,128)} %constant.178, f32[2,64,128,256,1]{3,1,0,2,4:T(8,128)} %bitcast.160), kind=kOutput, calls=%fused_computation.31 | convolution fusion | flops 805306368 | bytes 20971520 | tf_op jit(solution)/shard_map/ckqw,kqejcd->edjkw/dot_general | solution.py:289
  264.1 3.3 reshape.276
  267.4 4.0 copy.151
  271.4 21.4 %all-to-all-done.1 = f32[16,2,2,64,128]{4,2,1,3,0:T(2,128)S(1)} async-done(((f32[16,2,2,64,128]{4,2,1,3,0:T(2,128)}), f32[16,2,2,64,128]{4,2,1,3,0:T(2,128)S(1)}, u32[]{:S(2)}, u32[]{:S(2)}) %all-to-all-start.1) | async-done | bytes 2097184 | tf_op jit(solution)/shard_map/all_to_all | solution.py:291
  292.8 5.4 %all-to-all-start.3 = ((f32[16,2,2,64,128]{4,2,1,3,0:T(2,128)}), f32[16,2,2,64,128]{4,2,1,3,0:T(2,128)}, u32[]{:S(2)}, u32[]{:S(2)}) async-start(f32[16,2,2,64,128]{4,2,1,3,0:T(2,128)} %bitcast.167), calls=%async_computation.4 | async-start | bytes 4194304 | tf_op jit(solution)/shard_map/all_to_all | solution.py:291
  298.2 21.7 %fusion.19 = f32[16,2,2,64,256]{4,0,1,2,3:T(8,128)S(1)} fusion(f32[64,128,16,2,2,2]{1,2,4,5,3,0:T(8,128)} %constant.163.clone, f32[2,64,128,256,1,1]{3,1,0,2,5,4:T(8,128)} %bitcast.161), kind=kOutput, calls=%fused_computation.19 | convolution fusion | flops 1610612736 | bytes 25165824 | tf_op jit(solution)/shard_map/ckqw,kqejcd->edjkw/dot_general | solution.py:289
  319.9 4.4 copy.64
  324.3 6.2 %reshape.273 = f32[16,2,128,2,128]{4,3,2,1,0:T(2,128)} reshape(f32[16,2,2,64,256]{4,3,2,1,0:T(8,128)} %copy.64) | data formatting | bytes 8388608 | tf_op jit(solution)/shard_map/reshape | solution.py:290
  330.5 5.6 %copy.65 = f32[16,2,2,128,128]{4,2,1,3,0:T(2,128)} copy(f32[16,2,2,128,128]{4,2,3,1,0:T(2,128)} %bitcast.165) | data formatting | bytes 8388608 | tf_op jit(solution)/shard_map/transpose | solution.py:290
  336.1 10.3 %all-to-all-done.3 = f32[16,2,2,64,128]{4,2,1,3,0:T(2,128)} async-done(((f32[16,2,2,64,128]{4,2,1,3,0:T(2,128)}), f32[16,2,2,64,128]{4,2,1,3,0:T(2,128)}, u32[]{:S(2)}, u32[]{:S(2)}) %all-to-all-start.3) | async-done | bytes 2097184 | tf_op jit(solution)/shard_map/all_to_all | solution.py:291
  346.4 5.1 %all-to-all-start.2 = ((f32[16,2,2,128,128]{4,2,1,3,0:T(2,128)}), f32[16,2,2,128,128]{4,2,1,3,0:T(2,128)}, u32[]{:S(2)}, u32[]{:S(2)}) async-start(f32[16,2,2,128,128]{4,2,1,3,0:T(2,128)} %copy.65), calls=%async_computation.3 | async-start | bytes 8388608 | tf_op jit(solution)/shard_map/all_to_all | solution.py:291
  351.6 2.9 copy.103
  354.7 3.9 fusion.55
  358.9 2.9 convolution_bitcast_fusion.1
  361.8 4.5 fusion.35
  366.4 2.2 copy.61
  368.6 2.3 reshape.271
  370.9 4.6 convolution_bitcast_fusion
  375.5 4.5 fusion.38
  380.1 2.2 copy.73
  382.3 2.1 reshape.277
  384.5 1.8 multiply_divide_fusion.1
  386.3 1.8 copy.74
  388.1 3.2 copy.75
  391.3 53.0 %all-to-all-done.2 = f32[16,2,2,128,128]{4,2,1,3,0:T(2,128)} async-done(((f32[16,2,2,128,128]{4,2,1,3,0:T(2,128)}), f32[16,2,2,128,128]{4,2,1,3,0:T(2,128)}, u32[]{:S(2)}, u32[]{:S(2)}) %all-to-all-start.2) | async-done | bytes 4194336 | tf_op jit(solution)/shard_map/all_to_all | solution.py:291
  444.2 8.4 %fusion.16 = f32[2,64,128,128]{3,1,0,2:T(8,128)S(1)} fusion(f32[16,2,64,2,2,1]{2,0,1,3,4,5:T(8,128)S(1)} %copy-done.6, f32[16,2,2,128,128,1]{4,2,1,3,0,5:T(2,128)} %bitcast.57), kind=kOutput, calls=%fused_computation.18 | convolution fusion | flops 805306368 | bytes 12615680 | tf_op jit(solution)/shard_map/scnmq,snkcd->dkmq/dot_general | solution.py:292
  452.6 8.8 %fusion.26 = f32[128,64,64]{0,1,2:T(8,128)S(1)} fusion(f32[64,128,64,2]{1,2,3,0:T(8,128)S(1)} %copy-done.2, f32[2,64,128,128]{3,1,0,2:T(8,128)S(1)} %fusion.16), kind=kOutput, calls=%fused_computation.29 | convolution fusion | flops 805306368 | bytes 14680064 | tf_op jit(solution)/shard_map/ckmq,kqjc->mjk/dot_general | solution.py:293
  461.4 1.2 copy.68
  462.6 2.4 fusion.24
  465.0 3.7 maximum_bitcast_fusion
  468.7 5.6 %copy.76 = f32[1,256,4096]{2,1,0:T(8,128)} copy(f32[1,256,4096]{1,2,0:T(8,128)} %maximum_bitcast_fusion) | data formatting | bytes 8388608 | tf_op jit(solution)/shard_map/broadcast_in_dim | solution.py:301
  (62 shorter events, 6.6 us)
Async XLA Ops:
  6.5 21.1 %reduce-scatter.2.cloned.1.call-start = ((), (), s32[]{:S(2)}) async-start(), calls=%async_computation.6 | async-start | bytes 983040 | tf_op jit(solution)/shard_map/reduce_scatter | solution.py:220
  7.9 10.2 %copy-start.11 = (s32[1,2]{1,0:T(1,128)S(1)}, s32[1,2]{1,0:T(1,128)}, u32[]{:S(2)}) copy-start(s32[1,2]{1,0:T(1,128)} %param.27) | copy-start | bytes 28
  7.9 12.0 %copy-start.9 = (f32[1,8,2048]{2,1,0:T(8,128)S(1)}, f32[1,8,2048]{2,1,0:T(8,128)}, u32[]{:S(2)}) copy-start(f32[1,8,2048]{2,1,0:T(8,128)} %param.22) | copy-start | bytes 196612
  7.9 12.0 %copy-start.10 = (f32[1,8,2048]{2,1,0:T(8,128)S(1)}, f32[1,8,2048]{2,1,0:T(8,128)}, u32[]{:S(2)}) copy-start(f32[1,8,2048]{2,1,0:T(8,128)} %param.23) | copy-start | bytes 196612
  7.9 12.0 %copy-start.13 = (s32[1,128]{1,0:T(1,128)S(1)}, s32[1,128]{1,0:T(1,128)}, u32[]{:S(2)}) copy-start(s32[1,128]{1,0:T(1,128)} %param.25) | copy-start | bytes 1540
  7.9 12.0 %copy-start.14 = (s32[1,128,1]{1,2,0:T(1,128)S(1)}, s32[1,128,1]{1,2,0:T(1,128)}, u32[]{:S(2)}) copy-start(s32[1,128,1]{1,2,0:T(1,128)} %param.24) | copy-start | bytes 1540
  7.9 22.6 %copy-start.12 = (s32[1,128]{1,0:T(1,128)S(1)}, s32[1,128]{1,0:T(1,128)}, u32[]{:S(2)}) copy-start(s32[1,128]{1,0:T(1,128)} %param.26) | copy-start | bytes 1540
  32.5 142.4 %copy-start.7 = (f32[64,64,2,2,1]{0,1,2,3,4:T(8,128)S(1)}, f32[64,64,2,2,1]{0,1,2,3,4:T(8,128)}, u32[]{:S(2)}) copy-start(f32[64,64,2,2,1]{0,1,2,3,4:T(8,128)} %constant.179) | copy-start | bytes 196612
  32.5 38.3 %all-to-all-start = ((f32[16,40,512]{2,1,0:T(8,128)}), f32[16,40,512]{2,1,0:T(8,128)S(1)}, u32[]{:S(2)}, u32[]{:S(2)}) async-start(f32[16,40,512]{2,1,0:T(8,128)} %select_maximum_fusion), calls=%async_computation.1 | async-start | bytes 2621440 | tf_op jit(solution)/shard_map/all_to_all | solution.py:243
  174.8 25.8 %copy-start.4 = (f32[64,128,16,2,2]{1,2,3,4,0:T(8,128)S(1)}, f32[64,128,16,2,2]{1,2,3,4,0:T(8,128)}, u32[]{:S(2)}) copy-start(f32[64,128,16,2,2]{1,2,3,4,0:T(8,128)} %constant.177) | copy-start | bytes 6291460
  226.3 66.4 %all-to-all-start.1 = ((f32[16,2,2,64,128]{4,2,1,3,0:T(2,128)}), f32[16,2,2,64,128]{4,2,1,3,0:T(2,128)S(1)}, u32[]{:S(2)}, u32[]{:S(2)}) async-start(f32[16,2,2,64,128]{4,2,1,3,0:T(2,128)} %bitcast.168), calls=%async_computation.2 | async-start | bytes 4194304 | tf_op jit(solution)/shard_map/all_to_all | solution.py:291
  292.8 53.6 %all-to-all-start.3 = ((f32[16,2,2,64,128]{4,2,1,3,0:T(2,128)}), f32[16,2,2,64,128]{4,2,1,3,0:T(2,128)}, u32[]{:S(2)}, u32[]{:S(2)}) async-start(f32[16,2,2,64,128]{4,2,1,3,0:T(2,128)} %bitcast.167), calls=%async_computation.4 | async-start | bytes 4194304 | tf_op jit(solution)/shard_map/all_to_all | solution.py:291
  346.4 97.8 %all-to-all-start.2 = ((f32[16,2,2,128,128]{4,2,1,3,0:T(2,128)}), f32[16,2,2,128,128]{4,2,1,3,0:T(2,128)}, u32[]{:S(2)}, u32[]{:S(2)}) async-start(f32[16,2,2,128,128]{4,2,1,3,0:T(2,128)} %copy.65), calls=%async_computation.3 | async-start | bytes 8388608 | tf_op jit(solution)/shard_map/all_to_all | solution.py:291
  351.5 3.0 copy-start.8
  351.6 7.3 %copy-start.6 = (f32[16,2,64,2,2,1]{2,0,1,3,4,5:T(8,128)S(1)}, f32[16,2,64,2,2,1]{2,0,1,3,4,5:T(8,128)}, u32[]{:S(2)}) copy-start(f32[16,2,64,2,2,1]{2,0,1,3,4,5:T(8,128)} %constant.180) | copy-start | bytes 98308
  358.9 2.9 copy-start
  370.9 4.6 copy-start.1
  444.2 8.4 %copy-start.2 = (f32[64,128,64,2]{1,2,3,0:T(8,128)S(1)}, f32[64,128,64,2]{1,2,3,0:T(8,128)}, u32[]{:S(2)}) copy-start(f32[64,128,64,2]{1,2,3,0:T(8,128)} %constant.160.clone) | copy-start | bytes 12582916
  461.4 3.7 copy-start.3
Sparse Core Ops, SparseCore 0:
  18.2 9.4 reduce-scatter.1
